TPU v7x, 256 devices: a whole 4x4x8 slice. The times are simulated.
256 devices in a mesh: node: 256 (over z, x, y, core).
Axes of the slice: x: 4, y: 4, z: 8, core: 2. Of those that a mesh axis runs over, the one named last changes fastest.
Arguments:
- embed: float32 [1048576, 128], P('node')
- tiles: bfloat16 [49152, 128, 128], P('node'), may hold values from -0.21875 to 0.21875
- tile_rows: int32 [49152], P('node'), may hold values from 0 to 31
- tile_cols: int32 [49152], P('node'), may hold values from 0 to 8191, as said below
- tile_count: int32 [256], P('node'), may hold values from 48 to 192, as said below
Outputs:
- spectral: float32 [1048576, 128], P('node')
Inputs may be any that keep to these rules, and one draw needn't show every extreme that they name: `tile_cols`: slot s of device d names one of device d's own blocks, one of the last 16 blocks of device d - 1, or one of the first 16 blocks of device d + 1 (devices counted around the cycle); the first slot of every device names a block of device d - 1 and the second one of device d + 1. `tile_count`: some device has all 192 slots live.
All inputs are finite; a program needn't handle non-finite values.
Results may differ from a plain program's by a relative error of at most 0.003.
Values may be sent and summed in bfloat16 or wider, within the bound.
No kernel may reach another device: no remote copies, remote signals or barrier semaphores. Data moves between devices by JAX's collectives and lax.ppermute only.
A program may use at most 128 MiB of HBM per device.

v0:
```python
import jax
import jax.numpy as jnp
from jax import lax
from jax.experimental import pallas as pl
from jax.experimental.pallas import tpu as pltpu
from jax.sharding import PartitionSpec as P

BS = 128
OWN = 32
HALF = 16
SLOTS = 192
LISTLEN = 256
GROUP = 4
PANEL = 16
TILE_COPIES = 8
CHUNK = 4
LOW = BS // 2
MIB = 1024 * 1024

F32 = jnp.float32
BF16 = jnp.bfloat16

spectral_shift = 0.5
weight_zero = 0.6
weight_one = -0.9
weight_two = 0.45
c_embed = weight_zero - weight_two
c_sum = 2.0 * weight_two
c_first = weight_one - c_sum * spectral_shift


def vmem(*shape, dtype):
    return pltpu.VMEM(shape, dtype)


def in_vmem(array):
    return pltpu.with_memory_space_constraint(array, pltpu.VMEM)


def in_hbm(array):
    return pltpu.with_memory_space_constraint(array, pltpu.HBM)


V = pl.BlockSpec(memory_space=pltpu.VMEM)
S = pl.BlockSpec(memory_space=pltpu.SMEM)
H = pl.BlockSpec(memory_space=pl.ANY)
M = pl.BlockSpec(memory_space=pltpu.HBM)


def params(mib):
    return pltpu.CompilerParams(vmem_limit_bytes=mib * MIB)


def cost(flops, moved):
    return pl.CostEstimate(flops=flops, bytes_accessed=moved, transcendentals=0)


def which_list(bucket):
    return (bucket >= OWN).astype(jnp.int32) + (bucket >= OWN + HALF).astype(jnp.int32)


def columns_of(row):
    return jnp.broadcast_to(row, (row.shape[1], row.shape[1])).T


def slot_lists(tile_rows, tile_cols, device, count, flip, size):
    i32 = jnp.int32
    shape = (1, LISTLEN)
    core = device % 2
    local = tile_cols - device * OWN + HALF
    local = jnp.where(local < 0, local + OWN * size, local)
    local = jnp.where(local >= OWN * size, local - OWN * size, local)
    own = (local >= HALF) & (local < HALF + OWN)
    after = (local >= HALF + OWN).astype(i32)
    source = jnp.where(own, (local - HALF) ^ flip, local - 48 * after + HALF * (after ^ core))
    row = tile_rows ^ flip
    slots = lax.broadcasted_iota(i32, shape, 1)
    alive = slots < count
    bucket = jnp.where(alive, jnp.where(own, row, row + OWN), 2 * OWN)
    kind = which_list(bucket)
    code = (slots | (source << 8) | (row << 16)).astype(F32)

    square = (LISTLEN, LISTLEN)
    before = lax.broadcasted_iota(i32, square, 0) < lax.broadcasted_iota(i32, square, 1)
    bucket_f32 = bucket.astype(F32)
    same = columns_of(bucket_f32) == jnp.broadcast_to(bucket_f32, square)
    rank = jnp.sum(jnp.where(same & before, 1.0, 0.0), axis=0, keepdims=True)
    wide = (2 * OWN, LISTLEN)
    buckets = lax.broadcasted_iota(i32, wide, 0)
    here = jnp.broadcast_to(bucket, wide)
    pairs = jnp.sum(jnp.where(buckets == here, 1.0, 0.0), axis=1, keepdims=True)
    pairs = jnp.floor((pairs + 1.0) * 0.5)
    kinds = which_list(buckets)
    earlier = (buckets < here) & (kinds == jnp.broadcast_to(kind, wide))
    start = jnp.sum(jnp.where(earlier, 2.0 * pairs, 0.0), axis=0, keepdims=True)
    place = jnp.where(alive, start + rank + (kind * LISTLEN).astype(F32), -1.0)
    place, code = columns_of(place), columns_of(code)
    lanes = lax.broadcasted_iota(i32, square, 1).astype(F32)
    order = [
        SLOTS + jnp.sum(jnp.where(place == lanes + k * LISTLEN, code - SLOTS, 0.0), axis=0, keepdims=True)
        for k in range(3)
    ]
    field = lax.broadcasted_iota(i32, wide, 1)
    meta = jnp.sum(jnp.where(kinds == field - 1, pairs, 0.0), axis=0, keepdims=True)
    meta = jnp.where(slots == 0, flip, meta.astype(i32))
    return jnp.concatenate(order, axis=1).astype(i32), meta


def tile_sums(order, start, stop, source, tiles, total):
    def group(g, carry):
        products = []
        for u in range(GROUP):
            at = start + 2 * (g * GROUP + u)
            first, second = order[0, at], order[0, at + 1]
            wide = jnp.concatenate([tiles[first & 255], tiles[second & 255]], axis=1)
            tall = jnp.concatenate([source[(first >> 8) & 255], source[(second >> 8) & 255]], axis=0)
            products.append((first >> 16, jnp.dot(wide, tall, preferred_element_type=F32)))
        for row, product in products:
            total[row] += product
        return carry

    lax.fori_loop(0, (stop + GROUP - 1) // GROUP, group, 0)


def load_kernel(size, where, counts, rows, columns, embed, tiles, total, kept, inner, order, meta, slots, near_rows, near_columns, sem):
    device, count = where[0], counts[0]
    flip = (device % 2) * HALF
    part = SLOTS // TILE_COPIES
    tile_copies = [
        pltpu.make_async_copy(
            tiles.at[pl.ds(c * part, part)], kept.at[pl.ds(c * part, part)], sem.at[2 + c]
        )
        for c in range(TILE_COPIES)
    ]
    halves = [
        pltpu.make_async_copy(
            embed.at[pl.ds(h * HALF ^ flip, HALF)], total.at[pl.ds(h * HALF, HALF)], sem.at[h]
        )
        for h in range(2)
    ]
    slot_copies = [
        pltpu.make_async_copy(rows, near_rows, sem.at[2 + TILE_COPIES]),
        pltpu.make_async_copy(columns, near_columns, sem.at[3 + TILE_COPIES]),
    ]
    for copy in slot_copies + halves + tile_copies:
        copy.start()
    kept[SLOTS] = jnp.zeros((BS, BS), BF16)
    slots[...] = jnp.zeros_like(slots)
    for copy in slot_copies:
        copy.wait()
    slots[0:1, :SLOTS] = near_rows[...]
    slots[1:2, :SLOTS] = near_columns[...]
    order[...], meta[...] = slot_lists(slots[0:1, :], slots[1:2, :], device, count, flip, size)
    for copy in halves:
        copy.wait()
    inner[...] = total[HALF:].astype(BF16)
    total[...] = total[...] * (-spectral_shift)
    for copy in tile_copies:
        copy.wait()


def own_first_kernel(order, meta, cross, inner, tiles, before, total, source):
    source[:HALF] = cross[...]
    source[HALF:] = inner[...]
    tile_sums(order, 0, meta[0, 1], source, tiles, total)


def halo_first_cross_kernel(order, meta, cross, inner, tiles, before, total, source, out_cross):
    source[:HALF] = cross[...]
    source[HALF:] = inner[...]
    tile_sums(order, LISTLEN, meta[0, 2], source, tiles, total)
    out_cross[...] = total[:HALF].astype(BF16)


def own_second_kernel(order, meta, halo, cross, tiles, before, total, out_lower, out_upper, source):
    tile_sums(order, 2 * LISTLEN, meta[0, 3], halo, tiles, total)
    inner = total[HALF:].astype(BF16)
    out_lower[...] = inner[: HALF // 2]
    out_upper[...] = inner[HALF // 2 :]
    source[:HALF] = cross[...]
    source[HALF:] = inner
    total[...] = total[...] * (c_first / c_sum)
    tile_sums(order, 0, meta[0, 1], source, tiles, total)


def halo_second_kernel(order, meta, cross, lower, upper, tiles, before, embed, split, gram, source, total, field, sem):
    flip = meta[0, 0]
    halves = [
        pltpu.make_async_copy(
            embed.at[pl.ds(h * HALF ^ flip, HALF)], field.at[pl.ds(h * HALF, HALF)], sem.at[h]
        )
        for h in range(2)
    ]
    for copy in halves:
        copy.start()
    source[:HALF] = cross[...]
    source[HALF : HALF + HALF // 2] = lower[...]
    source[HALF + HALF // 2 :] = upper[...]
    total[...] = before[...]
    tile_sums(order, LISTLEN, meta[0, 2], source, tiles, total)
    tile_sums(order, 2 * LISTLEN, meta[0, 3], source, tiles, total)
    for copy in halves:
        copy.wait()

    sums = jnp.zeros((BS, 2 * BS), F32)
    for g in range(OWN // CHUNK):
        rows = pl.ds(g * CHUNK, CHUNK)
        mixed = (c_sum * total[rows] + c_embed * field[rows]).reshape(CHUNK * BS, BS)
        high = mixed.astype(BF16)
        low = (mixed - high.astype(F32)).astype(BF16)
        both = jnp.concatenate([high, low], axis=1)
        split[rows] = both.reshape(CHUNK, BS, 2 * BS)
        sums += lax.dot_general(high, both, (((0,), (0,)), ((), ())), preferred_element_type=F32)
    gram[...] = packed(sums[:, :BS] + (sums[:, BS:] + sums[:, BS:].T))


def packed(gram):
    row = lax.broadcasted_iota(jnp.int32, (LOW, BS), 0)
    column = lax.broadcasted_iota(jnp.int32, (LOW, BS), 1)
    lower = pltpu.roll(gram[LOW:], LOW, 1)
    body = jnp.where((column >= LOW) | (row <= column), gram[:LOW], lower)
    diagonal = jnp.sum(jnp.where(row == column, lower, 0.0), axis=0, keepdims=True)
    return jnp.concatenate([body, jnp.broadcast_to(diagonal, (8, BS))], axis=0)


def unpacked(pack):
    row = lax.broadcasted_iota(jnp.int32, (LOW, BS), 0)
    column = lax.broadcasted_iota(jnp.int32, (LOW, BS), 1)
    body = pack[:LOW]
    turned = jnp.concatenate([body, jnp.zeros((LOW, BS), F32)], axis=0).T
    upper = jnp.where((column >= LOW) | (row <= column), body, turned[:LOW])
    lower = jnp.where(row > column, body, jnp.where(row == column, pack[LOW : LOW + 1], turned[:LOW]))
    lower = jnp.where(column < LOW, turned[LOW:], pltpu.roll(lower, LOW, 1))
    return jnp.concatenate([upper, lower], axis=0)


def three_parts(x):
    high = x.astype(BF16)
    rest = x - high.astype(F32)
    middle = rest.astype(BF16)
    low = (rest - middle.astype(F32)).astype(BF16)
    return high, middle, low


def inverse_factor(gram, work):
    n = BS
    rows = lax.broadcasted_iota(jnp.int32, (n, n), 0)
    columns = lax.broadcasted_iota(jnp.int32, (n, n), 1)
    work[:, :n] = gram
    work[:, n:] = jnp.where(rows == columns, 1.0, 0.0).astype(F32)
    place = lax.broadcasted_iota(jnp.int32, (PANEL, n), 0)
    for base in range(0, n, PANEL):
        panel = work[base : base + PANEL, :]
        left, right = panel[:, :n], panel[:, n:]
        spread = [
            jnp.broadcast_to(left[:, base + k : base + k + 1], (PANEL, n)) for k in range(PANEL)
        ]
        scale = jnp.zeros((PANEL, n), F32)
        for j in range(PANEL):
            inverse = 1.0 / spread[j][j : j + 1, :]
            scale = jnp.where(place == j, inverse, scale)
            if j + 1 < PANEL:
                factor = jnp.where(place > j, spread[j] * inverse, 0.0)
                for k in range(j + 1, PANEL):
                    spread[k] = spread[k] - factor * spread[k][j : j + 1, :]
                left = left - factor * left[j : j + 1, :]
                right = right - factor * right[j : j + 1, :]
        if base + PANEL < n:
            ah, am, al = three_parts(left * scale)
            both = jnp.concatenate([left, right], axis=1)
            bh, bm, bl = three_parts(both)
            update = lax.dot_general(
                jnp.concatenate([ah, ah, am, am, ah, al], axis=0),
                jnp.concatenate([bh, bm, bh, bm, bl, bh], axis=0),
                (((0,), (0,)), ((), ())),
                preferred_element_type=F32,
            )
            work[base + PANEL :, :] -= update[base + PANEL :, :]
        work[base : base + PANEL, n:] = right * jnp.sqrt(scale)


def solve_kernel(total_rows, meta, gram, split, out, work, result, sem):
    flip = meta[0, 0]
    inverse_factor(unpacked(gram[...]), work)
    spread = (work[:, BS:] * jnp.sqrt(F32(total_rows))).T
    high = spread.astype(BF16)
    low = (spread - high.astype(F32)).astype(BF16)
    half = jnp.concatenate([high, low], axis=1)
    factor = jnp.concatenate([half, half], axis=0)
    steps = 8
    size = OWN // steps
    copies = []
    for step in range(steps):
        rows = split[step * size : (step + 1) * size].reshape(size * BS, 2 * BS)
        product = jnp.dot(rows, factor, preferred_element_type=F32)
        result[step * size : (step + 1) * size] = (product[:, :BS] + product[:, BS:]).reshape(size, BS, BS)
        copies.append(
            pltpu.make_async_copy(
                result.at[pl.ds(step * size, size)], out.at[pl.ds(step * size ^ flip, size)], sem.at[step]
            )
        )
        copies[-1].start()
    for copy in copies:
        copy.wait()


def swap(pairs, x):
    return lax.ppermute(x, "node", pairs)


def sum_over_node(x, size):
    for masks in ((1,), (2, 6, 4), (8, 24, 16), (32, 64, 96), (224,)):
        x = x + sum(swap([(i, i ^ mask) for i in range(size)], x) for mask in masks)
    return x


def local(embed, tiles, tile_rows, tile_cols, tile_count):
    size = lax.axis_size("node")
    device = lax.axis_index("node")
    flip = (device % 2) * HALF
    to_chip = [(i, (i + 1) % size if i % 2 else (i - 1) % size) for i in range(size)]
    to_core = [(i, i ^ 1) for i in range(size)]
    blocks = embed.reshape(OWN, BS, BS)

    cross = lax.dynamic_slice_in_dim(blocks, flip, HALF, 0).astype(BF16)
    cross_in = swap(to_chip, cross)
    where = device.astype(jnp.int32).reshape(1)

    def load(*refs):
        load_kernel(size, *refs)

    blocks_f32 = vmem(OWN, BS, BS, dtype=F32)
    source = vmem(OWN, BS, BS, dtype=BF16)
    half = vmem(HALF, BS, BS, dtype=BF16)
    work = cost(2 * 96 * BS**3, 8 * MIB)
    brief = cost(2 * BS**3, BS * BS)
    total, kept, inner, order, meta = pl.pallas_call(
        load,
        out_shape=(
            blocks_f32,
            vmem(SLOTS + 1, BS, BS, dtype=BF16),
            half,
            vmem(1, 3 * LISTLEN, dtype=jnp.int32),
            vmem(1, LISTLEN, dtype=jnp.int32),
        ),
        in_specs=[S, S, M, M, M, M],
        out_specs=(V, V, V, V, V),
        scratch_shapes=[
            vmem(8, LISTLEN, dtype=jnp.int32),
            vmem(1, SLOTS, dtype=jnp.int32),
            vmem(1, SLOTS, dtype=jnp.int32),
            pltpu.SemaphoreType.DMA((4 + TILE_COPIES,)),
        ],
        compiler_params=params(24),
        cost_estimate=work,
        name="load",
    )(where, tile_count, *map(in_hbm, (tile_rows.reshape(1, SLOTS), tile_cols.reshape(1, SLOTS), blocks, tiles)))
    inner_in = swap(to_core, inner)

    total = pl.pallas_call(
        own_first_kernel,
        out_shape=blocks_f32,
        in_specs=[S, S, V, V, V, V],
        out_specs=V,
        input_output_aliases={5: 0},
        scratch_shapes=[source],
        compiler_params=params(24),
        cost_estimate=work,
        name="own_first",
    )(order, meta, in_vmem(cross), in_vmem(inner), in_vmem(kept), in_vmem(total))

    total, halo, cross = pl.pallas_call(
        halo_first_cross_kernel,
        out_shape=(blocks_f32, source, half),
        in_specs=[S, S, V, V, V, V],
        out_specs=(V, V, V),
        input_output_aliases={5: 0},
        compiler_params=params(24),
        cost_estimate=work,
        name="halo_first_cross",
    )(order, meta, in_vmem(cross_in), in_vmem(inner_in), in_vmem(kept), in_vmem(total))
    cross_in = swap(to_chip, cross)

    quarter = vmem(HALF // 2, BS, BS, dtype=BF16)
    total, lower, upper = pl.pallas_call(
        own_second_kernel,
        out_shape=(blocks_f32, quarter, quarter),
        in_specs=[S, S, V, V, V, V],
        out_specs=(V, V, V),
        input_output_aliases={5: 0},
        scratch_shapes=[source],
        compiler_params=params(24),
        cost_estimate=brief,
        name="own_second",
    )(order, meta, in_vmem(halo), in_vmem(cross), in_vmem(kept), in_vmem(total))
    lower_in, upper_in = swap(to_core, lower), swap(to_core, upper)

    split, gram = pl.pallas_call(
        halo_second_kernel,
        out_shape=(vmem(OWN, BS, 2 * BS, dtype=BF16), vmem(LOW + 8, BS, dtype=F32)),
        in_specs=[S, S, V, V, V, V, V, H],
        out_specs=(V, V),
        scratch_shapes=[source, blocks_f32, blocks_f32, pltpu.SemaphoreType.DMA((2,))],
        compiler_params=params(24),
        cost_estimate=work,
        name="halo_second",
    )(order, meta, *map(in_vmem, (cross_in, lower_in, upper_in, kept, total)), blocks)

    gram = sum_over_node(gram, size)

    def solve(*refs):
        solve_kernel(embed.shape[0] * size, *refs)

    out = pl.pallas_call(
        solve,
        out_shape=jax.ShapeDtypeStruct((OWN, BS, BS), F32),
        in_specs=[S, V, V],
        out_specs=H,
        scratch_shapes=[vmem(BS, 2 * BS, dtype=F32), blocks_f32, pltpu.SemaphoreType.DMA((8,))],
        compiler_params=params(24),
        name="solve",
    )(meta, in_vmem(gram), in_vmem(split))
    return out.reshape(embed.shape)


def solution(mesh):
    return jax.shard_map(
        local,
        mesh=mesh,
        in_specs=(P("node", None), P("node", None, None), P("node"), P("node"), P("node")),
        out_specs=P("node", None),
        check_vma=False,
    )
```

profile of v0, /device:TPU:4, one launch (start us, length us, event | category | flops | bytes accessed | tf_op | source)
XLA Modules:
  0.0 72.7 jit_solution(2024345536807239919)
XLA Ops:
  0.0 1.3 %dynamic-slice_convert_fusion.cross = bf16[16,128,128]{2,1,0:T(8,128)(2,1)S(1)} fusion(f32[32,128,128]{2,1,0:T(8,128)} %bitcast.5, s32[]{:T(128)S(6)} %select_n.11), kind=kLoop, calls=%fused_computation | loop fusion | bytes 1048580 | tf_op jit(solution)/shard_map/convert_element_type | solution.py:325
  1.3 2.5 %collective-permute-start = (bf16[16,128,128]{2,1,0:T(8,128)(2,1)S(1)}, bf16[16,128,128]{2,1,0:T(8,128)(2,1)S(1)}, u32[]{:S(2)}, u32[]{:S(2)}) collective-permute-start(bf16[16,128,128]{2,1,0:T(8,128)(2,1)S(1)} %dynamic-slice_convert_fusion.cross), channel_id=1, source_target_pairs={{0,255},{1,2},{2,1},{3,4},{4,3},{5,6},{6,5},{7,8},{8,7},{9,10},{10... | collective-permute-start | bytes 1572872 | tf_op jit(solution)/shard_map/ppermute | solution.py:308
  4.5 3.5 %load.1 = (f32[32,128,128]{2,1,0:T(8,128)S(1)}, bf16[193,128,128]{2,1,0:T(8,128)(2,1)S(1)}, bf16[16,128,128]{2,1,0:T(8,128)(2,1)S(1)}, s32[1,768]{1,0:T(1,128)S(1)}, s32[1,256]{1,0:T(1,128)S(1)}) custom-call(s32[1]{0:T(128)} %bitcast.refs_0_, s32[1]{0:T(128)S(6)} %copy.12.refs_1_, s32[1,192]{1,0:T(1,128)} %bitcast.8, s32[1,192]{1,0:T(1,128)} %bitcast.9, ...), custom_call_target="tpu_custom_call" | custom-call | flops 402653184 | bytes 8388608 | tf_op jit(solution)/shard_map/load/pallas_call | solution.py:337
  8.0 0.1 collective-permute-start.1
  8.1 3.9 %own_first.1.before = f32[32,128,128]{2,1,0:T(8,128)S(1)} custom-call(s32[1,768]{1,0:T(1,128)S(1)} %get-tuple-element.19.order, s32[1,256]{1,0:T(1,128)S(1)} %get-tuple-element.18.meta.refs_0_, bf16[16,128,128]{2,1,0:T(8,128)(2,1)S(1)} %dynamic-slice_convert_fusion.cross, ...), custom_call_target="tpu_custom_call", output_to_operand_aliasing={{}: (5, {})} | custom-call | flops 402653184 | bytes 8388608 | tf_op jit(solution)/shard_map/own_first/pallas_call | solution.py:360
  12.0 0.1 collective-permute-done.cross
  12.1 0.0 collective-permute-done.1.inner
  12.1 2.3 %halo_first_cross.1 = (f32[32,128,128]{2,1,0:T(8,128)S(1)}, bf16[32,128,128]{2,1,0:T(8,128)(2,1)S(1)}, bf16[16,128,128]{2,1,0:T(8,128)(2,1)S(1)}) custom-call(s32[1,768]{1,0:T(1,128)S(1)} %get-tuple-element.19.order, s32[1,256]{1,0:T(1,128)S(1)} %get-tuple-element.18.meta.refs_0_, ...), custom_call_target="tpu_custom_call", output_to_operand_aliasing={{0}: (5, {})} | custom-call | flops 402653184 | bytes 8388608 | tf_op jit(solution)/shard_map/halo_first_cross/pallas_call | solution.py:372
  14.5 1.8 %collective-permute-start.2 = (bf16[16,128,128]{2,1,0:T(8,128)(2,1)S(1)}, bf16[16,128,128]{2,1,0:T(8,128)(2,1)S(1)}, u32[]{:S(2)}, u32[]{:S(2)}) collective-permute-start(bf16[16,128,128]{2,1,0:T(8,128)(2,1)S(1)} %get-tuple-element.23.cross), channel_id=1, source_target_pairs={{0,255},{1,2},{2,1},{3,4},{4,3},{5,6},{6,5},{7,8},{8,7},{9,10},{10... | collective-permute-start | bytes 1572872 | tf_op jit(solution)/shard_map/ppermute | solution.py:308
  16.3 0.0 copy-start
  16.3 5.9 %own_second.1 = (f32[32,128,128]{2,1,0:T(8,128)S(1)}, bf16[8,128,128]{2,1,0:T(8,128)(2,1)S(1)}, bf16[8,128,128]{2,1,0:T(8,128)(2,1)S(1)}) custom-call(s32[1,768]{1,0:T(1,128)S(1)} %get-tuple-element.19.order, s32[1,256]{1,0:T(1,128)S(1)} %get-tuple-element.18.meta.refs_0_, ...), custom_call_target="tpu_custom_call", output_to_operand_aliasing={{0}: (5, {})} | custom-call | flops 4194304 | bytes 16384 | tf_op jit(solution)/shard_map/own_second/pallas_call | solution.py:385
  22.2 0.1 collective-permute-start.3
  22.3 0.5 collective-permute-start.4
  22.8 1.0 %collective-permute-done.3.lower = bf16[8,128,128]{2,1,0:T(8,128)(2,1)S(1)} collective-permute-done((bf16[8,128,128]{2,1,0:T(8,128)(2,1)S(1)}, bf16[8,128,128]{2,1,0:T(8,128)(2,1)S(1)}, u32[]{:S(2)}, u32[]{:S(2)}) %collective-permute-start.3) | collective-permute-done | bytes 262176 | tf_op jit(solution)/shard_map/ppermute | solution.py:308
  23.8 0.4 collective-permute-done.4.upper
  24.2 1.1 %collective-permute-done.2.cross = bf16[16,128,128]{2,1,0:T(8,128)(2,1)S(1)} collective-permute-done((bf16[16,128,128]{2,1,0:T(8,128)(2,1)S(1)}, bf16[16,128,128]{2,1,0:T(8,128)(2,1)S(1)}, u32[]{:S(2)}, u32[]{:S(2)}) %collective-permute-start.2) | collective-permute-done | bytes 524320 | tf_op jit(solution)/shard_map/ppermute | solution.py:308
  25.3 0.0 copy-done
  25.3 5.4 %halo_second.1 = (bf16[32,128,256]{2,1,0:T(8,128)(2,1)S(1)}, f32[72,128]{1,0:T(8,128)S(1)}) custom-call(s32[1,768]{1,0:T(1,128)S(1)} %get-tuple-element.19.order, s32[1,256]{1,0:T(1,128)S(1)} %get-tuple-element.18.meta.refs_0_, bf16[16,128,128]{2,1,0:T(8,128)(2,1)S(1)} %collective-permute-done.2.cross, ...), custom_call_target="tpu_custom_call" | custom-call | flops 402653184 | bytes 8388608 | tf_op jit(solution)/shard_map/halo_second/pallas_call | solution.py:398
  30.6 0.1 collective-permute-start.5
  30.8 1.2 %collective-permute-done.5 = f32[72,128]{1,0:T(8,128)S(1)} collective-permute-done((f32[72,128]{1,0:T(8,128)S(1)}, f32[72,128]{1,0:T(8,128)S(1)}, u32[]{:S(2)}, u32[]{:S(2)}) %collective-permute-start.5) | collective-permute-done | bytes 36896 | tf_op jit(solution)/shard_map/ppermute | solution.py:308
  32.0 0.0 collective-permute-start.8
  32.0 1.9 %collective-permute-start.7 = (f32[72,128]{1,0:T(8,128)S(1)}, f32[72,128]{1,0:T(8,128)S(1)}, u32[]{:S(2)}, u32[]{:S(2)}) collective-permute-start(f32[72,128]{1,0:T(8,128)S(1)} %add.42), channel_id=1, source_target_pairs={{0,6},{1,7},{2,4},{3,5},{4,2},{5,3},{6,0},{7,1},{8,14},{9,15},{10,... | collective-permute-start | bytes 110600 | tf_op jit(solution)/shard_map/ppermute | solution.py:308
  33.9 1.6 %collective-permute-start.6 = (f32[72,128]{1,0:T(8,128)S(1)}, f32[72,128]{1,0:T(8,128)S(1)}, u32[]{:S(2)}, u32[]{:S(2)}) collective-permute-start(f32[72,128]{1,0:T(8,128)S(1)} %add.42), channel_id=1, source_target_pairs={{0,2},{1,3},{2,0},{3,1},{4,6},{5,7},{6,4},{7,5},{8,10},{9,11},{10,... | collective-permute-start | bytes 110600 | tf_op jit(solution)/shard_map/ppermute | solution.py:308
  35.4 2.1 %collective-permute-done.8 = f32[72,128]{1,0:T(8,128)S(1)} collective-permute-done((f32[72,128]{1,0:T(8,128)S(1)}, f32[72,128]{1,0:T(8,128)S(1)}, u32[]{:S(2)}, u32[]{:S(2)}) %collective-permute-start.8) | collective-permute-done | bytes 36896 | tf_op jit(solution)/shard_map/ppermute | solution.py:308
  37.5 0.1 collective-permute-done.7
  37.6 0.2 collective-permute-done.6
  37.8 10.7 %collective-permute-start.11 = (f32[72,128]{1,0:T(8,128)S(1)}, f32[72,128]{1,0:T(8,128)S(1)}, u32[]{:S(2)}, u32[]{:S(2)}) collective-permute-start(f32[72,128]{1,0:T(8,128)S(1)} %add_add_fusion.2), channel_id=1, source_target_pairs={{0,16},{1,17},{2,18},{3,19},{4,20},{5,21},{6,22},{7,23},{8,24},{9,... | collective-permute-start | bytes 110600 | tf_op jit(solution)/shard_map/ppermute | solution.py:308
  48.5 0.0 collective-permute-start.10
  48.5 1.3 %collective-permute-start.9 = (f32[72,128]{1,0:T(8,128)S(1)}, f32[72,128]{1,0:T(8,128)S(1)}, u32[]{:S(2)}, u32[]{:S(2)}) collective-permute-start(f32[72,128]{1,0:T(8,128)S(1)} %add_add_fusion.2), channel_id=1, source_target_pairs={{0,8},{1,9},{2,10},{3,11},{4,12},{5,13},{6,14},{7,15},{8,0},{9,1},... | collective-permute-start | bytes 110600 | tf_op jit(solution)/shard_map/ppermute | solution.py:308
  49.8 0.8 %collective-permute-done.11 = f32[72,128]{1,0:T(8,128)S(1)} collective-permute-done((f32[72,128]{1,0:T(8,128)S(1)}, f32[72,128]{1,0:T(8,128)S(1)}, u32[]{:S(2)}, u32[]{:S(2)}) %collective-permute-start.11) | collective-permute-done | bytes 36896 | tf_op jit(solution)/shard_map/ppermute | solution.py:308
  50.6 1.9 %collective-permute-done.10 = f32[72,128]{1,0:T(8,128)S(1)} collective-permute-done((f32[72,128]{1,0:T(8,128)S(1)}, f32[72,128]{1,0:T(8,128)S(1)}, u32[]{:S(2)}, u32[]{:S(2)}) %collective-permute-start.10) | collective-permute-done | bytes 36896 | tf_op jit(solution)/shard_map/ppermute | solution.py:308
  52.5 0.0 collective-permute-done.9
  52.5 0.9 %collective-permute-start.14 = (f32[72,128]{1,0:T(8,128)S(1)}, f32[72,128]{1,0:T(8,128)S(1)}, u32[]{:S(2)}, u32[]{:S(2)}) collective-permute-start(f32[72,128]{1,0:T(8,128)S(1)} %add_add_fusion.1), channel_id=1, source_target_pairs={{0,96},{1,97},{2,98},{3,99},{4,100},{5,101},{6,102},{7,103},{8,104... | collective-permute-start | bytes 110600 | tf_op jit(solution)/shard_map/ppermute | solution.py:308
  53.4 0.0 collective-permute-start.13
  53.4 3.6 %collective-permute-start.12 = (f32[72,128]{1,0:T(8,128)S(1)}, f32[72,128]{1,0:T(8,128)S(1)}, u32[]{:S(2)}, u32[]{:S(2)}) collective-permute-start(f32[72,128]{1,0:T(8,128)S(1)} %add_add_fusion.1), channel_id=1, source_target_pairs={{0,32},{1,33},{2,34},{3,35},{4,36},{5,37},{6,38},{7,39},{8,40},{9,... | collective-permute-start | bytes 110600 | tf_op jit(solution)/shard_map/ppermute | solution.py:308
  57.0 1.5 %collective-permute-done.14 = f32[72,128]{1,0:T(8,128)S(1)} collective-permute-done((f32[72,128]{1,0:T(8,128)S(1)}, f32[72,128]{1,0:T(8,128)S(1)}, u32[]{:S(2)}, u32[]{:S(2)}) %collective-permute-start.14) | collective-permute-done | bytes 36896 | tf_op jit(solution)/shard_map/ppermute | solution.py:308
  58.5 0.6 collective-permute-done.13
  59.1 0.0 collective-permute-done.12
  59.1 5.5 %collective-permute-start.15 = (f32[72,128]{1,0:T(8,128)S(1)}, f32[72,128]{1,0:T(8,128)S(1)}, u32[]{:S(2)}, u32[]{:S(2)}) collective-permute-start(f32[72,128]{1,0:T(8,128)S(1)} %add_add_fusion), channel_id=1, source_target_pairs={{0,224},{1,225},{2,226},{3,227},{4,228},{5,229},{6,230},{7,231},{8... | collective-permute-start | bytes 110600 | tf_op jit(solution)/shard_map/ppermute | solution.py:308
  64.7 1.9 %collective-permute-done.15 = f32[72,128]{1,0:T(8,128)S(1)} collective-permute-done((f32[72,128]{1,0:T(8,128)S(1)}, f32[72,128]{1,0:T(8,128)S(1)}, u32[]{:S(2)}, u32[]{:S(2)}) %collective-permute-start.15) | collective-permute-done | bytes 36896 | tf_op jit(solution)/shard_map/ppermute | solution.py:308
  66.6 6.0 %solve.1 = f32[32,128,128]{2,1,0:T(8,128)} custom-call(s32[1,256]{1,0:T(1,128)S(1)} %get-tuple-element.18.meta.refs_0_, f32[72,128]{1,0:T(8,128)S(1)} %add.52.refs_1_, bf16[32,128,256]{2,1,0:T(8,128)(2,1)S(1)} %get-tuple-element.30.refs_2_), custom_call_target="tpu_custom_call" | custom-call | tf_op jit(solution)/shard_map/solve/pallas_call | solution.py:414
  (5 shorter events, 0.0 us)
Async XLA Ops:
  1.3 10.8 %collective-permute-start = (bf16[16,128,128]{2,1,0:T(8,128)(2,1)S(1)}, bf16[16,128,128]{2,1,0:T(8,128)(2,1)S(1)}, u32[]{:S(2)}, u32[]{:S(2)}) collective-permute-start(bf16[16,128,128]{2,1,0:T(8,128)(2,1)S(1)} %dynamic-slice_convert_fusion.cross), channel_id=1, source_target_pairs={{0,255},{1,2},{2,1},{3,4},{4,3},{5,6},{6,5},{7,8},{8,7},{9,10},{10... | collective-permute-start | bytes 1572872 | tf_op jit(solution)/shard_map/ppermute | solution.py:308
  8.0 4.1 %collective-permute-start.1 = (bf16[16,128,128]{2,1,0:T(8,128)(2,1)S(1)}, bf16[16,128,128]{2,1,0:T(8,128)(2,1)S(1)}, u32[]{:S(2)}, u32[]{:S(2)}) collective-permute-start(bf16[16,128,128]{2,1,0:T(8,128)(2,1)S(1)} %get-tuple-element.20.inner), channel_id=1, source_target_pairs={{0,1},{1,0},{2,3},{3,2},{4,5},{5,4},{6,7},{7,6},{8,9},{9,8},{10,11... | collective-permute-start | bytes 1572872 | tf_op jit(solution)/shard_map/ppermute | solution.py:308
  14.5 10.8 %collective-permute-start.2 = (bf16[16,128,128]{2,1,0:T(8,128)(2,1)S(1)}, bf16[16,128,128]{2,1,0:T(8,128)(2,1)S(1)}, u32[]{:S(2)}, u32[]{:S(2)}) collective-permute-start(bf16[16,128,128]{2,1,0:T(8,128)(2,1)S(1)} %get-tuple-element.23.cross), channel_id=1, source_target_pairs={{0,255},{1,2},{2,1},{3,4},{4,3},{5,6},{6,5},{7,8},{8,7},{9,10},{10... | collective-permute-start | bytes 1572872 | tf_op jit(solution)/shard_map/ppermute | solution.py:308
  16.3 9.0 %copy-start = (f32[4096,128]{1,0:T(8,128)S(1)}, f32[4096,128]{1,0:T(8,128)}, u32[]{:S(2)}) copy-start(f32[4096,128]{1,0:T(8,128)} %param.5) | copy-start | bytes 6291460
  22.2 1.6 %collective-permute-start.3 = (bf16[8,128,128]{2,1,0:T(8,128)(2,1)S(1)}, bf16[8,128,128]{2,1,0:T(8,128)(2,1)S(1)}, u32[]{:S(2)}, u32[]{:S(2)}) collective-permute-start(bf16[8,128,128]{2,1,0:T(8,128)(2,1)S(1)} %get-tuple-element.26), channel_id=1, source_target_pairs={{0,1},{1,0},{2,3},{3,2},{4,5},{5,4},{6,7},{7,6},{8,9},{9,8},{10,11... | collective-permute-start | bytes 786440 | tf_op jit(solution)/shard_map/ppermute | solution.py:308
  22.3 1.9 %collective-permute-start.4 = (bf16[8,128,128]{2,1,0:T(8,128)(2,1)S(1)}, bf16[8,128,128]{2,1,0:T(8,128)(2,1)S(1)}, u32[]{:S(2)}, u32[]{:S(2)}) collective-permute-start(bf16[8,128,128]{2,1,0:T(8,128)(2,1)S(1)} %get-tuple-element.27), channel_id=1, source_target_pairs={{0,1},{1,0},{2,3},{3,2},{4,5},{5,4},{6,7},{7,6},{8,9},{9,8},{10,11... | collective-permute-start | bytes 786440 | tf_op jit(solution)/shard_map/ppermute | solution.py:308
  30.6 1.3 %collective-permute-start.5 = (f32[72,128]{1,0:T(8,128)S(1)}, f32[72,128]{1,0:T(8,128)S(1)}, u32[]{:S(2)}, u32[]{:S(2)}) collective-permute-start(f32[72,128]{1,0:T(8,128)S(1)} %get-tuple-element.29), channel_id=1, source_target_pairs={{0,1},{1,0},{2,3},{3,2},{4,5},{5,4},{6,7},{7,6},{8,9},{9,8},{10,11... | collective-permute-start | bytes 110600 | tf_op jit(solution)/shard_map/ppermute | solution.py:308
  32.0 5.6 %collective-permute-start.8 = (f32[72,128]{1,0:T(8,128)S(1)}, f32[72,128]{1,0:T(8,128)S(1)}, u32[]{:S(2)}, u32[]{:S(2)}) collective-permute-start(f32[72,128]{1,0:T(8,128)S(1)} %add.42), channel_id=1, source_target_pairs={{0,4},{1,5},{2,6},{3,7},{4,0},{5,1},{6,2},{7,3},{8,12},{9,13},{10,... | collective-permute-start | bytes 110600 | tf_op jit(solution)/shard_map/ppermute | solution.py:308
  32.0 5.7 %collective-permute-start.7 = (f32[72,128]{1,0:T(8,128)S(1)}, f32[72,128]{1,0:T(8,128)S(1)}, u32[]{:S(2)}, u32[]{:S(2)}) collective-permute-start(f32[72,128]{1,0:T(8,128)S(1)} %add.42), channel_id=1, source_target_pairs={{0,6},{1,7},{2,4},{3,5},{4,2},{5,3},{6,0},{7,1},{8,14},{9,15},{10,... | collective-permute-start | bytes 110600 | tf_op jit(solution)/shard_map/ppermute | solution.py:308
  33.9 4.0 %collective-permute-start.6 = (f32[72,128]{1,0:T(8,128)S(1)}, f32[72,128]{1,0:T(8,128)S(1)}, u32[]{:S(2)}, u32[]{:S(2)}) collective-permute-start(f32[72,128]{1,0:T(8,128)S(1)} %add.42), channel_id=1, source_target_pairs={{0,2},{1,3},{2,0},{3,1},{4,6},{5,7},{6,4},{7,5},{8,10},{9,11},{10,... | collective-permute-start | bytes 110600 | tf_op jit(solution)/shard_map/ppermute | solution.py:308
  37.8 12.8 %collective-permute-start.11 = (f32[72,128]{1,0:T(8,128)S(1)}, f32[72,128]{1,0:T(8,128)S(1)}, u32[]{:S(2)}, u32[]{:S(2)}) collective-permute-start(f32[72,128]{1,0:T(8,128)S(1)} %add_add_fusion.2), channel_id=1, source_target_pairs={{0,16},{1,17},{2,18},{3,19},{4,20},{5,21},{6,22},{7,23},{8,24},{9,... | collective-permute-start | bytes 110600 | tf_op jit(solution)/shard_map/ppermute | solution.py:308
  48.5 4.0 %collective-permute-start.10 = (f32[72,128]{1,0:T(8,128)S(1)}, f32[72,128]{1,0:T(8,128)S(1)}, u32[]{:S(2)}, u32[]{:S(2)}) collective-permute-start(f32[72,128]{1,0:T(8,128)S(1)} %add_add_fusion.2), channel_id=1, source_target_pairs={{0,24},{1,25},{2,26},{3,27},{4,28},{5,29},{6,30},{7,31},{8,16},{9,... | collective-permute-start | bytes 110600 | tf_op jit(solution)/shard_map/ppermute | solution.py:308
  48.5 4.0 %collective-permute-start.9 = (f32[72,128]{1,0:T(8,128)S(1)}, f32[72,128]{1,0:T(8,128)S(1)}, u32[]{:S(2)}, u32[]{:S(2)}) collective-permute-start(f32[72,128]{1,0:T(8,128)S(1)} %add_add_fusion.2), channel_id=1, source_target_pairs={{0,8},{1,9},{2,10},{3,11},{4,12},{5,13},{6,14},{7,15},{8,0},{9,1},... | collective-permute-start | bytes 110600 | tf_op jit(solution)/shard_map/ppermute | solution.py:308
  52.5 5.9 %collective-permute-start.14 = (f32[72,128]{1,0:T(8,128)S(1)}, f32[72,128]{1,0:T(8,128)S(1)}, u32[]{:S(2)}, u32[]{:S(2)}) collective-permute-start(f32[72,128]{1,0:T(8,128)S(1)} %add_add_fusion.1), channel_id=1, source_target_pairs={{0,96},{1,97},{2,98},{3,99},{4,100},{5,101},{6,102},{7,103},{8,104... | collective-permute-start | bytes 110600 | tf_op jit(solution)/shard_map/ppermute | solution.py:308
  53.4 5.7 %collective-permute-start.13 = (f32[72,128]{1,0:T(8,128)S(1)}, f32[72,128]{1,0:T(8,128)S(1)}, u32[]{:S(2)}, u32[]{:S(2)}) collective-permute-start(f32[72,128]{1,0:T(8,128)S(1)} %add_add_fusion.1), channel_id=1, source_target_pairs={{0,64},{1,65},{2,66},{3,67},{4,68},{5,69},{6,70},{7,71},{8,72},{9,... | collective-permute-start | bytes 110600 | tf_op jit(solution)/shard_map/ppermute | solution.py:308
  53.4 5.7 %collective-permute-start.12 = (f32[72,128]{1,0:T(8,128)S(1)}, f32[72,128]{1,0:T(8,128)S(1)}, u32[]{:S(2)}, u32[]{:S(2)}) collective-permute-start(f32[72,128]{1,0:T(8,128)S(1)} %add_add_fusion.1), channel_id=1, source_target_pairs={{0,32},{1,33},{2,34},{3,35},{4,36},{5,37},{6,38},{7,39},{8,40},{9,... | collective-permute-start | bytes 110600 | tf_op jit(solution)/shard_map/ppermute | solution.py:308
  59.1 7.5 %collective-permute-start.15 = (f32[72,128]{1,0:T(8,128)S(1)}, f32[72,128]{1,0:T(8,128)S(1)}, u32[]{:S(2)}, u32[]{:S(2)}) collective-permute-start(f32[72,128]{1,0:T(8,128)S(1)} %add_add_fusion), channel_id=1, source_target_pairs={{0,224},{1,225},{2,226},{3,227},{4,228},{5,229},{6,230},{7,231},{8... | collective-permute-start | bytes 110600 | tf_op jit(solution)/shard_map/ppermute | solution.py:308
where the time goes:
time: 72.9 us; the launch traced here: 72.7 us
  starting transfers between devices  30.6 us (42%)
  Pallas kernels  27 us (37%)
  waiting for transfers between devices  12.9 us (18%)
  local copies, waits for them, and re-layouts  1.31 us (2%)
  between operations  0.91 us (1%)
    ppermute x16, starting transfers between devices, swap(): return lax.ppermute(x, 'node', pairs)  30.6 us
    ppermute x16, waiting for transfers between devices, swap(): return lax.ppermute(x, 'node', pairs)  12.9 us
    pallas_call x1, Pallas kernels, local(): pl.pallas_call(solve, out_shape=jax.ShapeDtypeStruct((OWN, BS, BS), F32),...  5.95 us
    pallas_call x1, Pallas kernels, local(): pl.pallas_call(own_second_kernel, out_shape=(blocks_f32, quarter, quarter...  5.9 us
    pallas_call x1, Pallas kernels, local(): pl.pallas_call(halo_second_kernel, out_shape=(vmem(OWN, BS, 2 * BS, dtype...  5.37 us
    pallas_call x1, Pallas kernels, local(): pl.pallas_call(own_first_kernel, out_shape=blocks_f32, in_specs=[S, S, V,...  3.89 us
    pallas_call x1, Pallas kernels, local(): pl.pallas_call(load, out_shape=(blocks_f32, vmem(SLOTS + 1, BS, BS, dtype...  3.53 us
    pallas_call x1, Pallas kernels, local(): pl.pallas_call(halo_first_cross_kernel, out_shape=(blocks_f32, source, ha...  2.34 us
  transfers between devices with their start and end apart: 16, of which 13 were waited for; matrix products, arithmetic and copies ran while one was open for 0% of the time, Pallas kernels for 18%

commit v1 on v0

--- a/solution.py
+++ b/solution.py
@@ -10,7 +10,7 @@
 HALF = 16
 SLOTS = 192
 LISTLEN = 256
-GROUP = 4
+GROUP = 8
 PANEL = 16
 TILE_COPIES = 8
 CHUNK = 4
@@ -183,7 +183,7 @@
     tile_sums(order, 0, meta[0, 1], source, tiles, total)
 
 
-def halo_second_kernel(order, meta, cross, lower, upper, tiles, before, embed, split, gram, source, total, field, sem):
+def halo_second_kernel(order, meta, cross, lower, upper, tiles, before, embed, split, gram, total, source, field, sem):
     flip = meta[0, 0]
     halves = [
         pltpu.make_async_copy(
@@ -196,7 +196,6 @@
     source[:HALF] = cross[...]
     source[HALF : HALF + HALF // 2] = lower[...]
     source[HALF + HALF // 2 :] = upper[...]
-    total[...] = before[...]
     tile_sums(order, LISTLEN, meta[0, 2], source, tiles, total)
     tile_sums(order, 2 * LISTLEN, meta[0, 3], source, tiles, total)
     for copy in halves:
@@ -260,11 +259,11 @@
             inverse = 1.0 / spread[j][j : j + 1, :]
             scale = jnp.where(place == j, inverse, scale)
             if j + 1 < PANEL:
-                factor = jnp.where(place > j, spread[j] * inverse, 0.0)
+                column = jnp.where(place > j, spread[j], 0.0)
                 for k in range(j + 1, PANEL):
-                    spread[k] = spread[k] - factor * spread[k][j : j + 1, :]
-                left = left - factor * left[j : j + 1, :]
-                right = right - factor * right[j : j + 1, :]
+                    spread[k] = spread[k] - column * (spread[k][j : j + 1, :] * inverse)
+                left = left - column * (left[j : j + 1, :] * inverse)
+                right = right - column * (right[j : j + 1, :] * inverse)
         if base + PANEL < n:
             ah, am, al = three_parts(left * scale)
             both = jnp.concatenate([left, right], axis=1)
@@ -309,8 +308,22 @@
 
 
 def sum_over_node(x, size):
-    for masks in ((1,), (2, 6, 4), (8, 24, 16), (32, 64, 96), (224,)):
-        x = x + sum(swap([(i, i ^ mask) for i in range(size)], x) for mask in masks)
+    def masked(mask):
+        return [(i, i ^ mask) for i in range(size)]
+
+    def along_z(even, odd):
+        plane = 32
+        return [(i, (i + plane * (odd if i // plane % 2 else even)) % size) for i in range(size)]
+
+    rounds = (
+        (masked(1),),
+        (masked(2), masked(6), masked(4)),
+        (masked(8), masked(24), masked(16)),
+        (along_z(1, -1), along_z(-1, 1), along_z(-2, 2)),
+        (along_z(-3, 3),),
+    )
+    for pairs in rounds:
+        x = x + sum(swap(pair, x) for pair in pairs)
     return x
 
 
@@ -395,12 +408,13 @@
     )(order, meta, in_vmem(halo), in_vmem(cross), in_vmem(kept), in_vmem(total))
     lower_in, upper_in = swap(to_core, lower), swap(to_core, upper)
 
-    split, gram = pl.pallas_call(
+    split, gram, _ = pl.pallas_call(
         halo_second_kernel,
-        out_shape=(vmem(OWN, BS, 2 * BS, dtype=BF16), vmem(LOW + 8, BS, dtype=F32)),
+        out_shape=(vmem(OWN, BS, 2 * BS, dtype=BF16), vmem(LOW + 8, BS, dtype=F32), blocks_f32),
         in_specs=[S, S, V, V, V, V, V, H],
-        out_specs=(V, V),
-        scratch_shapes=[source, blocks_f32, blocks_f32, pltpu.SemaphoreType.DMA((2,))],
+        out_specs=(V, V, V),
+        input_output_aliases={6: 2},
+        scratch_shapes=[source, blocks_f32, pltpu.SemaphoreType.DMA((2,))],
         compiler_params=params(24),
         cost_estimate=work,
         name="halo_second",

time: 72.9 us -> 73.1 us (level)
  waiting for transfers between devices: 12.9 us -> 22.7 us
  Pallas kernels: 27 us -> 17.5 us
    ppermute x16, waiting for transfers between devices: 12.9 us -> 22.7 us  [swap(): return lax.ppermute(x, 'node', pairs)]
    pallas_call x1, Pallas kernels: 5.9 us -> 2.37 us  [local(): pl.pallas_call(own_second_kernel, out_shape=(blocks_f32, quarter, quarter...]
    pallas_call x1, Pallas kernels: 5.37 us -> 3.01 us  [local(): pl.pallas_call(halo_second_kernel, out_shape=(vmem(OWN, BS, 2 * BS, dtype...]
    pallas_call x1, Pallas kernels: 3.89 us -> 1.58 us  [local(): pl.pallas_call(own_first_kernel, out_shape=blocks_f32, in_specs=[S, S, V,...]
    pallas_call x1, Pallas kernels: 2.34 us -> 1.33 us  [local(): pl.pallas_call(halo_first_cross_kernel, out_shape=(blocks_f32, source, ha...]
  transfers between devices with their start and end apart: 16 -> 16, of which waited for: 13 -> 13; matrix products, arithmetic and copies ran while one was open for 0% -> 0% of each run, Pallas kernels for 18% -> 10%
where the time goes in v1:
time: 73.1 us; the launch traced here: 72.5 us
  starting transfers between devices  30.1 us (41%)
  waiting for transfers between devices  22.7 us (31%)
  Pallas kernels  17.5 us (24%)
  local copies, waits for them, and re-layouts  1.31 us (2%)
  between operations  0.91 us (1%)
    ppermute x16, starting transfers between devices, swap(): return lax.ppermute(x, 'node', pairs)  30.1 us
    ppermute x16, waiting for transfers between devices, swap(): return lax.ppermute(x, 'node', pairs)  22.7 us
    pallas_call x1, Pallas kernels, local(): pl.pallas_call(solve, out_shape=jax.ShapeDtypeStruct((OWN, BS, BS), F32),...  5.66 us
    pallas_call x1, Pallas kernels, local(): pl.pallas_call(load, out_shape=(blocks_f32, vmem(SLOTS + 1, BS, BS, dtype...  3.53 us
    pallas_call x1, Pallas kernels, local(): pl.pallas_call(halo_second_kernel, out_shape=(vmem(OWN, BS, 2 * BS, dtype...  3.01 us
    pallas_call x1, Pallas kernels, local(): pl.pallas_call(own_second_kernel, out_shape=(blocks_f32, quarter, quarter...  2.37 us
    pallas_call x1, Pallas kernels, local(): pl.pallas_call(own_first_kernel, out_shape=blocks_f32, in_specs=[S, S, V,...  1.58 us
  transfers between devices with their start and end apart: 16, of which 13 were waited for; matrix products, arithmetic and copies ran while one was open for 0% of the time, Pallas kernels for 10%

profile of v1, /device:TPU:4, one launch (start us, length us, event | category | flops | bytes accessed | tf_op | source)
XLA Modules:
  0.0 72.5 jit_solution(18041793837807588317)
XLA Ops:
  0.0 1.3 %dynamic-slice_convert_fusion.cross = bf16[16,128,128]{2,1,0:T(8,128)(2,1)S(1)} fusion(f32[32,128,128]{2,1,0:T(8,128)} %bitcast.5, s32[]{:T(128)S(6)} %select_n.11), kind=kLoop, calls=%fused_computation | loop fusion | bytes 1048580 | tf_op jit(solution)/shard_map/convert_element_type | solution.py:338
  1.3 2.5 %collective-permute-start = (bf16[16,128,128]{2,1,0:T(8,128)(2,1)S(1)}, bf16[16,128,128]{2,1,0:T(8,128)(2,1)S(1)}, u32[]{:S(2)}, u32[]{:S(2)}) collective-permute-start(bf16[16,128,128]{2,1,0:T(8,128)(2,1)S(1)} %dynamic-slice_convert_fusion.cross), channel_id=1, source_target_pairs={{0,255},{1,2},{2,1},{3,4},{4,3},{5,6},{6,5},{7,8},{8,7},{9,10},{10... | collective-permute-start | bytes 1572872 | tf_op jit(solution)/shard_map/ppermute | solution.py:307
  4.5 3.5 %load.1 = (f32[32,128,128]{2,1,0:T(8,128)S(1)}, bf16[193,128,128]{2,1,0:T(8,128)(2,1)S(1)}, bf16[16,128,128]{2,1,0:T(8,128)(2,1)S(1)}, s32[1,768]{1,0:T(1,128)S(1)}, s32[1,256]{1,0:T(1,128)S(1)}) custom-call(s32[1]{0:T(128)} %bitcast.refs_0_, s32[1]{0:T(128)S(6)} %copy.14.refs_1_, s32[1,192]{1,0:T(1,128)} %bitcast.8, s32[1,192]{1,0:T(1,128)} %bitcast.9, ...), custom_call_target="tpu_custom_call" | custom-call | flops 402653184 | bytes 8388608 | tf_op jit(solution)/shard_map/load/pallas_call | solution.py:350
  8.0 0.1 collective-permute-start.1
  8.1 1.6 %own_first.1.before = f32[32,128,128]{2,1,0:T(8,128)S(1)} custom-call(s32[1,768]{1,0:T(1,128)S(1)} %get-tuple-element.19.order, s32[1,256]{1,0:T(1,128)S(1)} %get-tuple-element.18.meta.refs_0_, bf16[16,128,128]{2,1,0:T(8,128)(2,1)S(1)} %dynamic-slice_convert_fusion.cross, ...), custom_call_target="tpu_custom_call", output_to_operand_aliasing={{}: (5, {})} | custom-call | flops 402653184 | bytes 8388608 | tf_op jit(solution)/shard_map/own_first/pallas_call | solution.py:373
  9.7 2.4 %collective-permute-done.cross = bf16[16,128,128]{2,1,0:T(8,128)(2,1)S(1)} collective-permute-done((bf16[16,128,128]{2,1,0:T(8,128)(2,1)S(1)}, bf16[16,128,128]{2,1,0:T(8,128)(2,1)S(1)}, u32[]{:S(2)}, u32[]{:S(2)}) %collective-permute-start) | collective-permute-done | bytes 524320 | tf_op jit(solution)/shard_map/ppermute | solution.py:307
  12.1 0.0 collective-permute-done.1.inner
  12.1 1.3 %halo_first_cross.1 = (f32[32,128,128]{2,1,0:T(8,128)S(1)}, bf16[32,128,128]{2,1,0:T(8,128)(2,1)S(1)}, bf16[16,128,128]{2,1,0:T(8,128)(2,1)S(1)}) custom-call(s32[1,768]{1,0:T(1,128)S(1)} %get-tuple-element.19.order, s32[1,256]{1,0:T(1,128)S(1)} %get-tuple-element.18.meta.refs_0_, ...), custom_call_target="tpu_custom_call", output_to_operand_aliasing={{0}: (5, {})} | custom-call | flops 402653184 | bytes 8388608 | tf_op jit(solution)/shard_map/halo_first_cross/pallas_call | solution.py:385
  13.5 2.8 %collective-permute-start.2 = (bf16[16,128,128]{2,1,0:T(8,128)(2,1)S(1)}, bf16[16,128,128]{2,1,0:T(8,128)(2,1)S(1)}, u32[]{:S(2)}, u32[]{:S(2)}) collective-permute-start(bf16[16,128,128]{2,1,0:T(8,128)(2,1)S(1)} %get-tuple-element.23.cross), channel_id=1, source_target_pairs={{0,255},{1,2},{2,1},{3,4},{4,3},{5,6},{6,5},{7,8},{8,7},{9,10},{10... | collective-permute-start | bytes 1572872 | tf_op jit(solution)/shard_map/ppermute | solution.py:307
  16.3 0.0 copy-start
  16.3 2.4 %own_second.1 = (f32[32,128,128]{2,1,0:T(8,128)S(1)}, bf16[8,128,128]{2,1,0:T(8,128)(2,1)S(1)}, bf16[8,128,128]{2,1,0:T(8,128)(2,1)S(1)}) custom-call(s32[1,768]{1,0:T(1,128)S(1)} %get-tuple-element.19.order, s32[1,256]{1,0:T(1,128)S(1)} %get-tuple-element.18.meta.refs_0_, ...), custom_call_target="tpu_custom_call", output_to_operand_aliasing={{0}: (5, {})} | custom-call | flops 4194304 | bytes 16384 | tf_op jit(solution)/shard_map/own_second/pallas_call | solution.py:398
  18.7 0.1 collective-permute-start.3
  18.8 0.5 collective-permute-start.4
  19.3 1.0 %collective-permute-done.3.lower = bf16[8,128,128]{2,1,0:T(8,128)(2,1)S(1)} collective-permute-done((bf16[8,128,128]{2,1,0:T(8,128)(2,1)S(1)}, bf16[8,128,128]{2,1,0:T(8,128)(2,1)S(1)}, u32[]{:S(2)}, u32[]{:S(2)}) %collective-permute-start.3) | collective-permute-done | bytes 262176 | tf_op jit(solution)/shard_map/ppermute | solution.py:307
  20.3 0.4 collective-permute-done.4.upper
  20.7 3.6 %collective-permute-done.2.cross = bf16[16,128,128]{2,1,0:T(8,128)(2,1)S(1)} collective-permute-done((bf16[16,128,128]{2,1,0:T(8,128)(2,1)S(1)}, bf16[16,128,128]{2,1,0:T(8,128)(2,1)S(1)}, u32[]{:S(2)}, u32[]{:S(2)}) %collective-permute-start.2) | collective-permute-done | bytes 524320 | tf_op jit(solution)/shard_map/ppermute | solution.py:307
  24.3 0.0 copy-done
  24.3 3.0 %halo_second.1 = (bf16[32,128,256]{2,1,0:T(8,128)(2,1)S(1)}, f32[72,128]{1,0:T(8,128)S(1)}, f32[32,128,128]{2,1,0:T(8,128)S(1)}) custom-call(s32[1,768]{1,0:T(1,128)S(1)} %get-tuple-element.19.order, s32[1,256]{1,0:T(1,128)S(1)} %get-tuple-element.18.meta.refs_0_, ...), custom_call_target="tpu_custom_call", output_to_operand_aliasing={{2}: (6, {})} | custom-call | flops 402653184 | bytes 8388608 | tf_op jit(solution)/shard_map/halo_second/pallas_call | solution.py:411
  27.3 0.1 collective-permute-start.5
  27.4 1.2 %collective-permute-done.5 = f32[72,128]{1,0:T(8,128)S(1)} collective-permute-done((f32[72,128]{1,0:T(8,128)S(1)}, f32[72,128]{1,0:T(8,128)S(1)}, u32[]{:S(2)}, u32[]{:S(2)}) %collective-permute-start.5) | collective-permute-done | bytes 36896 | tf_op jit(solution)/shard_map/ppermute | solution.py:307
  28.6 0.0 collective-permute-start.8
  28.6 2.6 %collective-permute-start.7 = (f32[72,128]{1,0:T(8,128)S(1)}, f32[72,128]{1,0:T(8,128)S(1)}, u32[]{:S(2)}, u32[]{:S(2)}) collective-permute-start(f32[72,128]{1,0:T(8,128)S(1)} %add.42), channel_id=1, source_target_pairs={{0,6},{1,7},{2,4},{3,5},{4,2},{5,3},{6,0},{7,1},{8,14},{9,15},{10,... | collective-permute-start | bytes 110600 | tf_op jit(solution)/shard_map/ppermute | solution.py:307
  31.2 0.9 %collective-permute-start.6 = (f32[72,128]{1,0:T(8,128)S(1)}, f32[72,128]{1,0:T(8,128)S(1)}, u32[]{:S(2)}, u32[]{:S(2)}) collective-permute-start(f32[72,128]{1,0:T(8,128)S(1)} %add.42), channel_id=1, source_target_pairs={{0,2},{1,3},{2,0},{3,1},{4,6},{5,7},{6,4},{7,5},{8,10},{9,11},{10,... | collective-permute-start | bytes 110600 | tf_op jit(solution)/shard_map/ppermute | solution.py:307
  32.1 2.0 %collective-permute-done.8 = f32[72,128]{1,0:T(8,128)S(1)} collective-permute-done((f32[72,128]{1,0:T(8,128)S(1)}, f32[72,128]{1,0:T(8,128)S(1)}, u32[]{:S(2)}, u32[]{:S(2)}) %collective-permute-start.8) | collective-permute-done | bytes 36896 | tf_op jit(solution)/shard_map/ppermute | solution.py:307
  34.1 0.2 collective-permute-done.7
  34.3 0.9 %collective-permute-done.6 = f32[72,128]{1,0:T(8,128)S(1)} collective-permute-done((f32[72,128]{1,0:T(8,128)S(1)}, f32[72,128]{1,0:T(8,128)S(1)}, u32[]{:S(2)}, u32[]{:S(2)}) %collective-permute-start.6) | collective-permute-done | bytes 36896 | tf_op jit(solution)/shard_map/ppermute | solution.py:307
  35.2 9.5 %collective-permute-start.11 = (f32[72,128]{1,0:T(8,128)S(1)}, f32[72,128]{1,0:T(8,128)S(1)}, u32[]{:S(2)}, u32[]{:S(2)}) collective-permute-start(f32[72,128]{1,0:T(8,128)S(1)} %add_add_fusion.2), channel_id=1, source_target_pairs={{0,16},{1,17},{2,18},{3,19},{4,20},{5,21},{6,22},{7,23},{8,24},{9,... | collective-permute-start | bytes 110600 | tf_op jit(solution)/shard_map/ppermute | solution.py:307
  44.6 0.0 collective-permute-start.10
  44.6 1.3 %collective-permute-start.9 = (f32[72,128]{1,0:T(8,128)S(1)}, f32[72,128]{1,0:T(8,128)S(1)}, u32[]{:S(2)}, u32[]{:S(2)}) collective-permute-start(f32[72,128]{1,0:T(8,128)S(1)} %add_add_fusion.2), channel_id=1, source_target_pairs={{0,8},{1,9},{2,10},{3,11},{4,12},{5,13},{6,14},{7,15},{8,0},{9,1},... | collective-permute-start | bytes 110600 | tf_op jit(solution)/shard_map/ppermute | solution.py:307
  45.9 0.8 %collective-permute-done.11 = f32[72,128]{1,0:T(8,128)S(1)} collective-permute-done((f32[72,128]{1,0:T(8,128)S(1)}, f32[72,128]{1,0:T(8,128)S(1)}, u32[]{:S(2)}, u32[]{:S(2)}) %collective-permute-start.11) | collective-permute-done | bytes 36896 | tf_op jit(solution)/shard_map/ppermute | solution.py:307
  46.7 1.9 %collective-permute-done.10 = f32[72,128]{1,0:T(8,128)S(1)} collective-permute-done((f32[72,128]{1,0:T(8,128)S(1)}, f32[72,128]{1,0:T(8,128)S(1)}, u32[]{:S(2)}, u32[]{:S(2)}) %collective-permute-start.10) | collective-permute-done | bytes 36896 | tf_op jit(solution)/shard_map/ppermute | solution.py:307
  48.6 0.0 collective-permute-done.9
  48.6 4.8 %collective-permute-start.14 = (f32[72,128]{1,0:T(8,128)S(1)}, f32[72,128]{1,0:T(8,128)S(1)}, u32[]{:S(2)}, u32[]{:S(2)}) collective-permute-start(f32[72,128]{1,0:T(8,128)S(1)} %add_add_fusion.1), channel_id=1, source_target_pairs={{0,192},{1,193},{2,194},{3,195},{4,196},{5,197},{6,198},{7,199},{8... | collective-permute-start | bytes 110600 | tf_op jit(solution)/shard_map/ppermute | solution.py:307
  53.4 2.1 %collective-permute-start.13 = (f32[72,128]{1,0:T(8,128)S(1)}, f32[72,128]{1,0:T(8,128)S(1)}, u32[]{:S(2)}, u32[]{:S(2)}) collective-permute-start(f32[72,128]{1,0:T(8,128)S(1)} %add_add_fusion.1), channel_id=1, source_target_pairs={{0,224},{1,225},{2,226},{3,227},{4,228},{5,229},{6,230},{7,231},{8... | collective-permute-start | bytes 110600 | tf_op jit(solution)/shard_map/ppermute | solution.py:307
  55.5 0.0 collective-permute-start.12
  55.5 0.0 collective-permute-done.14
  55.5 3.1 %collective-permute-done.13 = f32[72,128]{1,0:T(8,128)S(1)} collective-permute-done((f32[72,128]{1,0:T(8,128)S(1)}, f32[72,128]{1,0:T(8,128)S(1)}, u32[]{:S(2)}, u32[]{:S(2)}) %collective-permute-start.13) | collective-permute-done | bytes 36896 | tf_op jit(solution)/shard_map/ppermute | solution.py:307
  58.6 0.9 %collective-permute-done.12 = f32[72,128]{1,0:T(8,128)S(1)} collective-permute-done((f32[72,128]{1,0:T(8,128)S(1)}, f32[72,128]{1,0:T(8,128)S(1)}, u32[]{:S(2)}, u32[]{:S(2)}) %collective-permute-start.12) | collective-permute-done | bytes 36896 | tf_op jit(solution)/shard_map/ppermute | solution.py:307
  59.4 2.9 %collective-permute-start.15 = (f32[72,128]{1,0:T(8,128)S(1)}, f32[72,128]{1,0:T(8,128)S(1)}, u32[]{:S(2)}, u32[]{:S(2)}) collective-permute-start(f32[72,128]{1,0:T(8,128)S(1)} %add_add_fusion), channel_id=1, source_target_pairs={{0,160},{1,161},{2,162},{3,163},{4,164},{5,165},{6,166},{7,167},{8... | collective-permute-start | bytes 110600 | tf_op jit(solution)/shard_map/ppermute | solution.py:307
  62.3 4.3 %collective-permute-done.15 = f32[72,128]{1,0:T(8,128)S(1)} collective-permute-done((f32[72,128]{1,0:T(8,128)S(1)}, f32[72,128]{1,0:T(8,128)S(1)}, u32[]{:S(2)}, u32[]{:S(2)}) %collective-permute-start.15) | collective-permute-done | bytes 36896 | tf_op jit(solution)/shard_map/ppermute | solution.py:307
  66.7 5.7 %solve.1 = f32[32,128,128]{2,1,0:T(8,128)} custom-call(s32[1,256]{1,0:T(1,128)S(1)} %get-tuple-element.18.meta.refs_0_, f32[72,128]{1,0:T(8,128)S(1)} %add.52.refs_1_, bf16[32,128,256]{2,1,0:T(8,128)(2,1)S(1)} %get-tuple-element.30.refs_2_), custom_call_target="tpu_custom_call" | custom-call | tf_op jit(solution)/shard_map/solve/pallas_call | solution.py:428
  (5 shorter events, 0.0 us)
Async XLA Ops:
  1.3 10.8 %collective-permute-start = (bf16[16,128,128]{2,1,0:T(8,128)(2,1)S(1)}, bf16[16,128,128]{2,1,0:T(8,128)(2,1)S(1)}, u32[]{:S(2)}, u32[]{:S(2)}) collective-permute-start(bf16[16,128,128]{2,1,0:T(8,128)(2,1)S(1)} %dynamic-slice_convert_fusion.cross), channel_id=1, source_target_pairs={{0,255},{1,2},{2,1},{3,4},{4,3},{5,6},{6,5},{7,8},{8,7},{9,10},{10... | collective-permute-start | bytes 1572872 | tf_op jit(solution)/shard_map/ppermute | solution.py:307
  8.0 4.1 %collective-permute-start.1 = (bf16[16,128,128]{2,1,0:T(8,128)(2,1)S(1)}, bf16[16,128,128]{2,1,0:T(8,128)(2,1)S(1)}, u32[]{:S(2)}, u32[]{:S(2)}) collective-permute-start(bf16[16,128,128]{2,1,0:T(8,128)(2,1)S(1)} %get-tuple-element.20.inner), channel_id=1, source_target_pairs={{0,1},{1,0},{2,3},{3,2},{4,5},{5,4},{6,7},{7,6},{8,9},{9,8},{10,11... | collective-permute-start | bytes 1572872 | tf_op jit(solution)/shard_map/ppermute | solution.py:307
  13.5 10.8 %collective-permute-start.2 = (bf16[16,128,128]{2,1,0:T(8,128)(2,1)S(1)}, bf16[16,128,128]{2,1,0:T(8,128)(2,1)S(1)}, u32[]{:S(2)}, u32[]{:S(2)}) collective-permute-start(bf16[16,128,128]{2,1,0:T(8,128)(2,1)S(1)} %get-tuple-element.23.cross), channel_id=1, source_target_pairs={{0,255},{1,2},{2,1},{3,4},{4,3},{5,6},{6,5},{7,8},{8,7},{9,10},{10... | collective-permute-start | bytes 1572872 | tf_op jit(solution)/shard_map/ppermute | solution.py:307
  16.3 8.0 %copy-start = (f32[4096,128]{1,0:T(8,128)S(1)}, f32[4096,128]{1,0:T(8,128)}, u32[]{:S(2)}) copy-start(f32[4096,128]{1,0:T(8,128)} %param.5) | copy-start | bytes 6291460
  18.7 1.6 %collective-permute-start.3 = (bf16[8,128,128]{2,1,0:T(8,128)(2,1)S(1)}, bf16[8,128,128]{2,1,0:T(8,128)(2,1)S(1)}, u32[]{:S(2)}, u32[]{:S(2)}) collective-permute-start(bf16[8,128,128]{2,1,0:T(8,128)(2,1)S(1)} %get-tuple-element.26), channel_id=1, source_target_pairs={{0,1},{1,0},{2,3},{3,2},{4,5},{5,4},{6,7},{7,6},{8,9},{9,8},{10,11... | collective-permute-start | bytes 786440 | tf_op jit(solution)/shard_map/ppermute | solution.py:307
  18.8 1.9 %collective-permute-start.4 = (bf16[8,128,128]{2,1,0:T(8,128)(2,1)S(1)}, bf16[8,128,128]{2,1,0:T(8,128)(2,1)S(1)}, u32[]{:S(2)}, u32[]{:S(2)}) collective-permute-start(bf16[8,128,128]{2,1,0:T(8,128)(2,1)S(1)} %get-tuple-element.27), channel_id=1, source_target_pairs={{0,1},{1,0},{2,3},{3,2},{4,5},{5,4},{6,7},{7,6},{8,9},{9,8},{10,11... | collective-permute-start | bytes 786440 | tf_op jit(solution)/shard_map/ppermute | solution.py:307
  27.3 1.3 %collective-permute-start.5 = (f32[72,128]{1,0:T(8,128)S(1)}, f32[72,128]{1,0:T(8,128)S(1)}, u32[]{:S(2)}, u32[]{:S(2)}) collective-permute-start(f32[72,128]{1,0:T(8,128)S(1)} %get-tuple-element.29), channel_id=1, source_target_pairs={{0,1},{1,0},{2,3},{3,2},{4,5},{5,4},{6,7},{7,6},{8,9},{9,8},{10,11... | collective-permute-start | bytes 110600 | tf_op jit(solution)/shard_map/ppermute | solution.py:307
  28.6 5.5 %collective-permute-start.8 = (f32[72,128]{1,0:T(8,128)S(1)}, f32[72,128]{1,0:T(8,128)S(1)}, u32[]{:S(2)}, u32[]{:S(2)}) collective-permute-start(f32[72,128]{1,0:T(8,128)S(1)} %add.42), channel_id=1, source_target_pairs={{0,4},{1,5},{2,6},{3,7},{4,0},{5,1},{6,2},{7,3},{8,12},{9,13},{10,... | collective-permute-start | bytes 110600 | tf_op jit(solution)/shard_map/ppermute | solution.py:307
  28.6 5.7 %collective-permute-start.7 = (f32[72,128]{1,0:T(8,128)S(1)}, f32[72,128]{1,0:T(8,128)S(1)}, u32[]{:S(2)}, u32[]{:S(2)}) collective-permute-start(f32[72,128]{1,0:T(8,128)S(1)} %add.42), channel_id=1, source_target_pairs={{0,6},{1,7},{2,4},{3,5},{4,2},{5,3},{6,0},{7,1},{8,14},{9,15},{10,... | collective-permute-start | bytes 110600 | tf_op jit(solution)/shard_map/ppermute | solution.py:307
  31.2 4.0 %collective-permute-start.6 = (f32[72,128]{1,0:T(8,128)S(1)}, f32[72,128]{1,0:T(8,128)S(1)}, u32[]{:S(2)}, u32[]{:S(2)}) collective-permute-start(f32[72,128]{1,0:T(8,128)S(1)} %add.42), channel_id=1, source_target_pairs={{0,2},{1,3},{2,0},{3,1},{4,6},{5,7},{6,4},{7,5},{8,10},{9,11},{10,... | collective-permute-start | bytes 110600 | tf_op jit(solution)/shard_map/ppermute | solution.py:307
  35.2 11.5 %collective-permute-start.11 = (f32[72,128]{1,0:T(8,128)S(1)}, f32[72,128]{1,0:T(8,128)S(1)}, u32[]{:S(2)}, u32[]{:S(2)}) collective-permute-start(f32[72,128]{1,0:T(8,128)S(1)} %add_add_fusion.2), channel_id=1, source_target_pairs={{0,16},{1,17},{2,18},{3,19},{4,20},{5,21},{6,22},{7,23},{8,24},{9,... | collective-permute-start | bytes 110600 | tf_op jit(solution)/shard_map/ppermute | solution.py:307
  44.6 4.0 %collective-permute-start.10 = (f32[72,128]{1,0:T(8,128)S(1)}, f32[72,128]{1,0:T(8,128)S(1)}, u32[]{:S(2)}, u32[]{:S(2)}) collective-permute-start(f32[72,128]{1,0:T(8,128)S(1)} %add_add_fusion.2), channel_id=1, source_target_pairs={{0,24},{1,25},{2,26},{3,27},{4,28},{5,29},{6,30},{7,31},{8,16},{9,... | collective-permute-start | bytes 110600 | tf_op jit(solution)/shard_map/ppermute | solution.py:307
  44.6 4.0 %collective-permute-start.9 = (f32[72,128]{1,0:T(8,128)S(1)}, f32[72,128]{1,0:T(8,128)S(1)}, u32[]{:S(2)}, u32[]{:S(2)}) collective-permute-start(f32[72,128]{1,0:T(8,128)S(1)} %add_add_fusion.2), channel_id=1, source_target_pairs={{0,8},{1,9},{2,10},{3,11},{4,12},{5,13},{6,14},{7,15},{8,0},{9,1},... | collective-permute-start | bytes 110600 | tf_op jit(solution)/shard_map/ppermute | solution.py:307
  48.6 6.9 %collective-permute-start.14 = (f32[72,128]{1,0:T(8,128)S(1)}, f32[72,128]{1,0:T(8,128)S(1)}, u32[]{:S(2)}, u32[]{:S(2)}) collective-permute-start(f32[72,128]{1,0:T(8,128)S(1)} %add_add_fusion.1), channel_id=1, source_target_pairs={{0,192},{1,193},{2,194},{3,195},{4,196},{5,197},{6,198},{7,199},{8... | collective-permute-start | bytes 110600 | tf_op jit(solution)/shard_map/ppermute | solution.py:307
  53.4 5.2 %collective-permute-start.13 = (f32[72,128]{1,0:T(8,128)S(1)}, f32[72,128]{1,0:T(8,128)S(1)}, u32[]{:S(2)}, u32[]{:S(2)}) collective-permute-start(f32[72,128]{1,0:T(8,128)S(1)} %add_add_fusion.1), channel_id=1, source_target_pairs={{0,224},{1,225},{2,226},{3,227},{4,228},{5,229},{6,230},{7,231},{8... | collective-permute-start | bytes 110600 | tf_op jit(solution)/shard_map/ppermute | solution.py:307
  55.5 4.0 %collective-permute-start.12 = (f32[72,128]{1,0:T(8,128)S(1)}, f32[72,128]{1,0:T(8,128)S(1)}, u32[]{:S(2)}, u32[]{:S(2)}) collective-permute-start(f32[72,128]{1,0:T(8,128)S(1)} %add_add_fusion.1), channel_id=1, source_target_pairs={{0,32},{1,33},{2,34},{3,35},{4,36},{5,37},{6,38},{7,39},{8,40},{9,... | collective-permute-start | bytes 110600 | tf_op jit(solution)/shard_map/ppermute | solution.py:307
  59.4 7.2 %collective-permute-start.15 = (f32[72,128]{1,0:T(8,128)S(1)}, f32[72,128]{1,0:T(8,128)S(1)}, u32[]{:S(2)}, u32[]{:S(2)}) collective-permute-start(f32[72,128]{1,0:T(8,128)S(1)} %add_add_fusion), channel_id=1, source_target_pairs={{0,160},{1,161},{2,162},{3,163},{4,164},{5,165},{6,166},{7,167},{8... | collective-permute-start | bytes 110600 | tf_op jit(solution)/shard_map/ppermute | solution.py:307

commit v2 on v1

--- a/solution.py
+++ b/solution.py
@@ -13,7 +13,7 @@
 GROUP = 8
 PANEL = 16
 TILE_COPIES = 8
-CHUNK = 4
+CHUNK = 8
 LOW = BS // 2
 MIB = 1024 * 1024
 

time: 73.1 us -> 73.4 us (level)
  transfers between devices with their start and end apart: 16 -> 16, of which waited for: 13 -> 13; matrix products, arithmetic and copies ran while one was open for 0% -> 0% of each run, Pallas kernels for 10% -> 11%
where the time goes in v2:
time: 73.4 us; the launch traced here: 73.1 us
  starting transfers between devices  30 us (41%)
  waiting for transfers between devices  22.7 us (31%)
  Pallas kernels  18.1 us (25%)
  local copies, waits for them, and re-layouts  1.31 us (2%)
  between operations  0.9 us (1%)
    ppermute x16, starting transfers between devices, swap(): return lax.ppermute(x, 'node', pairs)  30 us
    ppermute x16, waiting for transfers between devices, swap(): return lax.ppermute(x, 'node', pairs)  22.7 us
    pallas_call x1, Pallas kernels, local(): pl.pallas_call(solve, out_shape=jax.ShapeDtypeStruct((OWN, BS, BS), F32),...  5.66 us
    pallas_call x1, Pallas kernels, local(): pl.pallas_call(load, out_shape=(blocks_f32, vmem(SLOTS + 1, BS, BS, dtype...  3.53 us
    pallas_call x1, Pallas kernels, local(): pl.pallas_call(halo_second_kernel, out_shape=(vmem(OWN, BS, 2 * BS, dtype...  3.01 us
    pallas_call x1, Pallas kernels, local(): pl.pallas_call(own_second_kernel, out_shape=(blocks_f32, quarter, quarter...  2.68 us
    pallas_call x1, Pallas kernels, local(): pl.pallas_call(own_first_kernel, out_shape=blocks_f32, in_specs=[S, S, V,...  1.89 us
  transfers between devices with their start and end apart: 16, of which 13 were waited for; matrix products, arithmetic and copies ran while one was open for 0% of the time, Pallas kernels for 11%

profile of v2, /device:TPU:4, one launch (start us, length us, event | category | flops | bytes accessed | tf_op | source)
XLA Modules:
  0.0 73.1 jit_solution(9800751312784036889)
XLA Ops:
  0.0 1.3 %dynamic-slice_convert_fusion.cross = bf16[16,128,128]{2,1,0:T(8,128)(2,1)S(1)} fusion(f32[32,128,128]{2,1,0:T(8,128)} %bitcast.5, s32[]{:T(128)S(6)} %select_n.11), kind=kLoop, calls=%fused_computation | loop fusion | bytes 1048580 | tf_op jit(solution)/shard_map/convert_element_type | solution.py:338
  1.3 2.5 %collective-permute-start = (bf16[16,128,128]{2,1,0:T(8,128)(2,1)S(1)}, bf16[16,128,128]{2,1,0:T(8,128)(2,1)S(1)}, u32[]{:S(2)}, u32[]{:S(2)}) collective-permute-start(bf16[16,128,128]{2,1,0:T(8,128)(2,1)S(1)} %dynamic-slice_convert_fusion.cross), channel_id=1, source_target_pairs={{0,255},{1,2},{2,1},{3,4},{4,3},{5,6},{6,5},{7,8},{8,7},{9,10},{10... | collective-permute-start | bytes 1572872 | tf_op jit(solution)/shard_map/ppermute | solution.py:307
  4.5 3.5 %load.1 = (f32[32,128,128]{2,1,0:T(8,128)S(1)}, bf16[193,128,128]{2,1,0:T(8,128)(2,1)S(1)}, bf16[16,128,128]{2,1,0:T(8,128)(2,1)S(1)}, s32[1,768]{1,0:T(1,128)S(1)}, s32[1,256]{1,0:T(1,128)S(1)}) custom-call(s32[1]{0:T(128)} %bitcast.refs_0_, s32[1]{0:T(128)S(6)} %copy.14.refs_1_, s32[1,192]{1,0:T(1,128)} %bitcast.8, s32[1,192]{1,0:T(1,128)} %bitcast.9, ...), custom_call_target="tpu_custom_call" | custom-call | flops 402653184 | bytes 8388608 | tf_op jit(solution)/shard_map/load/pallas_call | solution.py:350
  8.0 0.1 collective-permute-start.1
  8.1 1.9 %own_first.1.before = f32[32,128,128]{2,1,0:T(8,128)S(1)} custom-call(s32[1,768]{1,0:T(1,128)S(1)} %get-tuple-element.19.order, s32[1,256]{1,0:T(1,128)S(1)} %get-tuple-element.18.meta.refs_0_, bf16[16,128,128]{2,1,0:T(8,128)(2,1)S(1)} %dynamic-slice_convert_fusion.cross, ...), custom_call_target="tpu_custom_call", output_to_operand_aliasing={{}: (5, {})} | custom-call | flops 402653184 | bytes 8388608 | tf_op jit(solution)/shard_map/own_first/pallas_call | solution.py:373
  10.0 2.1 %collective-permute-done.cross = bf16[16,128,128]{2,1,0:T(8,128)(2,1)S(1)} collective-permute-done((bf16[16,128,128]{2,1,0:T(8,128)(2,1)S(1)}, bf16[16,128,128]{2,1,0:T(8,128)(2,1)S(1)}, u32[]{:S(2)}, u32[]{:S(2)}) %collective-permute-start) | collective-permute-done | bytes 524320 | tf_op jit(solution)/shard_map/ppermute | solution.py:307
  12.1 0.0 collective-permute-done.1.inner
  12.1 1.3 %halo_first_cross.1 = (f32[32,128,128]{2,1,0:T(8,128)S(1)}, bf16[32,128,128]{2,1,0:T(8,128)(2,1)S(1)}, bf16[16,128,128]{2,1,0:T(8,128)(2,1)S(1)}) custom-call(s32[1,768]{1,0:T(1,128)S(1)} %get-tuple-element.19.order, s32[1,256]{1,0:T(1,128)S(1)} %get-tuple-element.18.meta.refs_0_, ...), custom_call_target="tpu_custom_call", output_to_operand_aliasing={{0}: (5, {})} | custom-call | flops 402653184 | bytes 8388608 | tf_op jit(solution)/shard_map/halo_first_cross/pallas_call | solution.py:385
  13.5 2.5 %collective-permute-start.2 = (bf16[16,128,128]{2,1,0:T(8,128)(2,1)S(1)}, bf16[16,128,128]{2,1,0:T(8,128)(2,1)S(1)}, u32[]{:S(2)}, u32[]{:S(2)}) collective-permute-start(bf16[16,128,128]{2,1,0:T(8,128)(2,1)S(1)} %get-tuple-element.23.cross), channel_id=1, source_target_pairs={{0,255},{1,2},{2,1},{3,4},{4,3},{5,6},{6,5},{7,8},{8,7},{9,10},{10... | collective-permute-start | bytes 1572872 | tf_op jit(solution)/shard_map/ppermute | solution.py:307
  16.0 0.0 copy-start
  16.0 2.7 %own_second.1 = (f32[32,128,128]{2,1,0:T(8,128)S(1)}, bf16[8,128,128]{2,1,0:T(8,128)(2,1)S(1)}, bf16[8,128,128]{2,1,0:T(8,128)(2,1)S(1)}) custom-call(s32[1,768]{1,0:T(1,128)S(1)} %get-tuple-element.19.order, s32[1,256]{1,0:T(1,128)S(1)} %get-tuple-element.18.meta.refs_0_, ...), custom_call_target="tpu_custom_call", output_to_operand_aliasing={{0}: (5, {})} | custom-call | flops 4194304 | bytes 16384 | tf_op jit(solution)/shard_map/own_second/pallas_call | solution.py:398
  18.7 0.1 collective-permute-start.3
  18.8 0.5 collective-permute-start.4
  19.3 1.0 %collective-permute-done.3.lower = bf16[8,128,128]{2,1,0:T(8,128)(2,1)S(1)} collective-permute-done((bf16[8,128,128]{2,1,0:T(8,128)(2,1)S(1)}, bf16[8,128,128]{2,1,0:T(8,128)(2,1)S(1)}, u32[]{:S(2)}, u32[]{:S(2)}) %collective-permute-start.3) | collective-permute-done | bytes 262176 | tf_op jit(solution)/shard_map/ppermute | solution.py:307
  20.3 0.4 collective-permute-done.4.upper
  20.7 3.6 %collective-permute-done.2.cross = bf16[16,128,128]{2,1,0:T(8,128)(2,1)S(1)} collective-permute-done((bf16[16,128,128]{2,1,0:T(8,128)(2,1)S(1)}, bf16[16,128,128]{2,1,0:T(8,128)(2,1)S(1)}, u32[]{:S(2)}, u32[]{:S(2)}) %collective-permute-start.2) | collective-permute-done | bytes 524320 | tf_op jit(solution)/shard_map/ppermute | solution.py:307
  24.3 0.0 copy-done
  24.3 3.0 %halo_second.1 = (bf16[32,128,256]{2,1,0:T(8,128)(2,1)S(1)}, f32[72,128]{1,0:T(8,128)S(1)}, f32[32,128,128]{2,1,0:T(8,128)S(1)}) custom-call(s32[1,768]{1,0:T(1,128)S(1)} %get-tuple-element.19.order, s32[1,256]{1,0:T(1,128)S(1)} %get-tuple-element.18.meta.refs_0_, ...), custom_call_target="tpu_custom_call", output_to_operand_aliasing={{2}: (6, {})} | custom-call | flops 402653184 | bytes 8388608 | tf_op jit(solution)/shard_map/halo_second/pallas_call | solution.py:411
  27.3 0.1 collective-permute-start.5
  27.4 1.2 %collective-permute-done.5 = f32[72,128]{1,0:T(8,128)S(1)} collective-permute-done((f32[72,128]{1,0:T(8,128)S(1)}, f32[72,128]{1,0:T(8,128)S(1)}, u32[]{:S(2)}, u32[]{:S(2)}) %collective-permute-start.5) | collective-permute-done | bytes 36896 | tf_op jit(solution)/shard_map/ppermute | solution.py:307
  28.6 0.7 collective-permute-start.8
  29.3 1.9 %collective-permute-start.7 = (f32[72,128]{1,0:T(8,128)S(1)}, f32[72,128]{1,0:T(8,128)S(1)}, u32[]{:S(2)}, u32[]{:S(2)}) collective-permute-start(f32[72,128]{1,0:T(8,128)S(1)} %add.42), channel_id=1, source_target_pairs={{0,6},{1,7},{2,4},{3,5},{4,2},{5,3},{6,0},{7,1},{8,14},{9,15},{10,... | collective-permute-start | bytes 110600 | tf_op jit(solution)/shard_map/ppermute | solution.py:307
  31.2 0.9 %collective-permute-start.6 = (f32[72,128]{1,0:T(8,128)S(1)}, f32[72,128]{1,0:T(8,128)S(1)}, u32[]{:S(2)}, u32[]{:S(2)}) collective-permute-start(f32[72,128]{1,0:T(8,128)S(1)} %add.42), channel_id=1, source_target_pairs={{0,2},{1,3},{2,0},{3,1},{4,6},{5,7},{6,4},{7,5},{8,10},{9,11},{10,... | collective-permute-start | bytes 110600 | tf_op jit(solution)/shard_map/ppermute | solution.py:307
  32.1 2.0 %collective-permute-done.8 = f32[72,128]{1,0:T(8,128)S(1)} collective-permute-done((f32[72,128]{1,0:T(8,128)S(1)}, f32[72,128]{1,0:T(8,128)S(1)}, u32[]{:S(2)}, u32[]{:S(2)}) %collective-permute-start.8) | collective-permute-done | bytes 36896 | tf_op jit(solution)/shard_map/ppermute | solution.py:307
  34.1 0.4 collective-permute-done.7
  34.4 0.7 collective-permute-done.6
  35.2 10.4 %collective-permute-start.11 = (f32[72,128]{1,0:T(8,128)S(1)}, f32[72,128]{1,0:T(8,128)S(1)}, u32[]{:S(2)}, u32[]{:S(2)}) collective-permute-start(f32[72,128]{1,0:T(8,128)S(1)} %add_add_fusion.2), channel_id=1, source_target_pairs={{0,16},{1,17},{2,18},{3,19},{4,20},{5,21},{6,22},{7,23},{8,24},{9,... | collective-permute-start | bytes 110600 | tf_op jit(solution)/shard_map/ppermute | solution.py:307
  45.5 0.0 collective-permute-start.10
  45.5 1.3 %collective-permute-start.9 = (f32[72,128]{1,0:T(8,128)S(1)}, f32[72,128]{1,0:T(8,128)S(1)}, u32[]{:S(2)}, u32[]{:S(2)}) collective-permute-start(f32[72,128]{1,0:T(8,128)S(1)} %add_add_fusion.2), channel_id=1, source_target_pairs={{0,8},{1,9},{2,10},{3,11},{4,12},{5,13},{6,14},{7,15},{8,0},{9,1},... | collective-permute-start | bytes 110600 | tf_op jit(solution)/shard_map/ppermute | solution.py:307
  46.8 0.8 %collective-permute-done.11 = f32[72,128]{1,0:T(8,128)S(1)} collective-permute-done((f32[72,128]{1,0:T(8,128)S(1)}, f32[72,128]{1,0:T(8,128)S(1)}, u32[]{:S(2)}, u32[]{:S(2)}) %collective-permute-start.11) | collective-permute-done | bytes 36896 | tf_op jit(solution)/shard_map/ppermute | solution.py:307
  47.6 1.9 %collective-permute-done.10 = f32[72,128]{1,0:T(8,128)S(1)} collective-permute-done((f32[72,128]{1,0:T(8,128)S(1)}, f32[72,128]{1,0:T(8,128)S(1)}, u32[]{:S(2)}, u32[]{:S(2)}) %collective-permute-start.10) | collective-permute-done | bytes 36896 | tf_op jit(solution)/shard_map/ppermute | solution.py:307
  49.5 0.0 collective-permute-done.9
  49.5 3.9 %collective-permute-start.14 = (f32[72,128]{1,0:T(8,128)S(1)}, f32[72,128]{1,0:T(8,128)S(1)}, u32[]{:S(2)}, u32[]{:S(2)}) collective-permute-start(f32[72,128]{1,0:T(8,128)S(1)} %add_add_fusion.1), channel_id=1, source_target_pairs={{0,192},{1,193},{2,194},{3,195},{4,196},{5,197},{6,198},{7,199},{8... | collective-permute-start | bytes 110600 | tf_op jit(solution)/shard_map/ppermute | solution.py:307
  53.4 2.7 %collective-permute-start.13 = (f32[72,128]{1,0:T(8,128)S(1)}, f32[72,128]{1,0:T(8,128)S(1)}, u32[]{:S(2)}, u32[]{:S(2)}) collective-permute-start(f32[72,128]{1,0:T(8,128)S(1)} %add_add_fusion.1), channel_id=1, source_target_pairs={{0,224},{1,225},{2,226},{3,227},{4,228},{5,229},{6,230},{7,231},{8... | collective-permute-start | bytes 110600 | tf_op jit(solution)/shard_map/ppermute | solution.py:307
  56.1 0.0 collective-permute-start.12
  56.1 0.0 collective-permute-done.14
  56.1 2.5 %collective-permute-done.13 = f32[72,128]{1,0:T(8,128)S(1)} collective-permute-done((f32[72,128]{1,0:T(8,128)S(1)}, f32[72,128]{1,0:T(8,128)S(1)}, u32[]{:S(2)}, u32[]{:S(2)}) %collective-permute-start.13) | collective-permute-done | bytes 36896 | tf_op jit(solution)/shard_map/ppermute | solution.py:307
  58.6 1.5 %collective-permute-done.12 = f32[72,128]{1,0:T(8,128)S(1)} collective-permute-done((f32[72,128]{1,0:T(8,128)S(1)}, f32[72,128]{1,0:T(8,128)S(1)}, u32[]{:S(2)}, u32[]{:S(2)}) %collective-permute-start.12) | collective-permute-done | bytes 36896 | tf_op jit(solution)/shard_map/ppermute | solution.py:307
  60.0 2.5 %collective-permute-start.15 = (f32[72,128]{1,0:T(8,128)S(1)}, f32[72,128]{1,0:T(8,128)S(1)}, u32[]{:S(2)}, u32[]{:S(2)}) collective-permute-start(f32[72,128]{1,0:T(8,128)S(1)} %add_add_fusion), channel_id=1, source_target_pairs={{0,160},{1,161},{2,162},{3,163},{4,164},{5,165},{6,166},{7,167},{8... | collective-permute-start | bytes 110600 | tf_op jit(solution)/shard_map/ppermute | solution.py:307
  62.6 4.7 %collective-permute-done.15 = f32[72,128]{1,0:T(8,128)S(1)} collective-permute-done((f32[72,128]{1,0:T(8,128)S(1)}, f32[72,128]{1,0:T(8,128)S(1)}, u32[]{:S(2)}, u32[]{:S(2)}) %collective-permute-start.15) | collective-permute-done | bytes 36896 | tf_op jit(solution)/shard_map/ppermute | solution.py:307
  67.3 5.7 %solve.1 = f32[32,128,128]{2,1,0:T(8,128)} custom-call(s32[1,256]{1,0:T(1,128)S(1)} %get-tuple-element.18.meta.refs_0_, f32[72,128]{1,0:T(8,128)S(1)} %add.52.refs_1_, bf16[32,128,256]{2,1,0:T(8,128)(2,1)S(1)} %get-tuple-element.30.refs_2_), custom_call_target="tpu_custom_call" | custom-call | tf_op jit(solution)/shard_map/solve/pallas_call | solution.py:428
  (5 shorter events, 0.1 us)
Async XLA Ops:
  1.3 10.8 %collective-permute-start = (bf16[16,128,128]{2,1,0:T(8,128)(2,1)S(1)}, bf16[16,128,128]{2,1,0:T(8,128)(2,1)S(1)}, u32[]{:S(2)}, u32[]{:S(2)}) collective-permute-start(bf16[16,128,128]{2,1,0:T(8,128)(2,1)S(1)} %dynamic-slice_convert_fusion.cross), channel_id=1, source_target_pairs={{0,255},{1,2},{2,1},{3,4},{4,3},{5,6},{6,5},{7,8},{8,7},{9,10},{10... | collective-permute-start | bytes 1572872 | tf_op jit(solution)/shard_map/ppermute | solution.py:307
  8.0 4.1 %collective-permute-start.1 = (bf16[16,128,128]{2,1,0:T(8,128)(2,1)S(1)}, bf16[16,128,128]{2,1,0:T(8,128)(2,1)S(1)}, u32[]{:S(2)}, u32[]{:S(2)}) collective-permute-start(bf16[16,128,128]{2,1,0:T(8,128)(2,1)S(1)} %get-tuple-element.20.inner), channel_id=1, source_target_pairs={{0,1},{1,0},{2,3},{3,2},{4,5},{5,4},{6,7},{7,6},{8,9},{9,8},{10,11... | collective-permute-start | bytes 1572872 | tf_op jit(solution)/shard_map/ppermute | solution.py:307
  13.5 10.8 %collective-permute-start.2 = (bf16[16,128,128]{2,1,0:T(8,128)(2,1)S(1)}, bf16[16,128,128]{2,1,0:T(8,128)(2,1)S(1)}, u32[]{:S(2)}, u32[]{:S(2)}) collective-permute-start(bf16[16,128,128]{2,1,0:T(8,128)(2,1)S(1)} %get-tuple-element.23.cross), channel_id=1, source_target_pairs={{0,255},{1,2},{2,1},{3,4},{4,3},{5,6},{6,5},{7,8},{8,7},{9,10},{10... | collective-permute-start | bytes 1572872 | tf_op jit(solution)/shard_map/ppermute | solution.py:307
  16.0 8.3 %copy-start = (f32[4096,128]{1,0:T(8,128)S(1)}, f32[4096,128]{1,0:T(8,128)}, u32[]{:S(2)}) copy-start(f32[4096,128]{1,0:T(8,128)} %param.5) | copy-start | bytes 6291460
  18.7 1.6 %collective-permute-start.3 = (bf16[8,128,128]{2,1,0:T(8,128)(2,1)S(1)}, bf16[8,128,128]{2,1,0:T(8,128)(2,1)S(1)}, u32[]{:S(2)}, u32[]{:S(2)}) collective-permute-start(bf16[8,128,128]{2,1,0:T(8,128)(2,1)S(1)} %get-tuple-element.26), channel_id=1, source_target_pairs={{0,1},{1,0},{2,3},{3,2},{4,5},{5,4},{6,7},{7,6},{8,9},{9,8},{10,11... | collective-permute-start | bytes 786440 | tf_op jit(solution)/shard_map/ppermute | solution.py:307
  18.8 1.9 %collective-permute-start.4 = (bf16[8,128,128]{2,1,0:T(8,128)(2,1)S(1)}, bf16[8,128,128]{2,1,0:T(8,128)(2,1)S(1)}, u32[]{:S(2)}, u32[]{:S(2)}) collective-permute-start(bf16[8,128,128]{2,1,0:T(8,128)(2,1)S(1)} %get-tuple-element.27), channel_id=1, source_target_pairs={{0,1},{1,0},{2,3},{3,2},{4,5},{5,4},{6,7},{7,6},{8,9},{9,8},{10,11... | collective-permute-start | bytes 786440 | tf_op jit(solution)/shard_map/ppermute | solution.py:307
  27.3 1.3 %collective-permute-start.5 = (f32[72,128]{1,0:T(8,128)S(1)}, f32[72,128]{1,0:T(8,128)S(1)}, u32[]{:S(2)}, u32[]{:S(2)}) collective-permute-start(f32[72,128]{1,0:T(8,128)S(1)} %get-tuple-element.29), channel_id=1, source_target_pairs={{0,1},{1,0},{2,3},{3,2},{4,5},{5,4},{6,7},{7,6},{8,9},{9,8},{10,11... | collective-permute-start | bytes 110600 | tf_op jit(solution)/shard_map/ppermute | solution.py:307
  28.6 5.5 %collective-permute-start.8 = (f32[72,128]{1,0:T(8,128)S(1)}, f32[72,128]{1,0:T(8,128)S(1)}, u32[]{:S(2)}, u32[]{:S(2)}) collective-permute-start(f32[72,128]{1,0:T(8,128)S(1)} %add.42), channel_id=1, source_target_pairs={{0,4},{1,5},{2,6},{3,7},{4,0},{5,1},{6,2},{7,3},{8,12},{9,13},{10,... | collective-permute-start | bytes 110600 | tf_op jit(solution)/shard_map/ppermute | solution.py:307
  29.3 5.2 %collective-permute-start.7 = (f32[72,128]{1,0:T(8,128)S(1)}, f32[72,128]{1,0:T(8,128)S(1)}, u32[]{:S(2)}, u32[]{:S(2)}) collective-permute-start(f32[72,128]{1,0:T(8,128)S(1)} %add.42), channel_id=1, source_target_pairs={{0,6},{1,7},{2,4},{3,5},{4,2},{5,3},{6,0},{7,1},{8,14},{9,15},{10,... | collective-permute-start | bytes 110600 | tf_op jit(solution)/shard_map/ppermute | solution.py:307
  31.2 4.0 %collective-permute-start.6 = (f32[72,128]{1,0:T(8,128)S(1)}, f32[72,128]{1,0:T(8,128)S(1)}, u32[]{:S(2)}, u32[]{:S(2)}) collective-permute-start(f32[72,128]{1,0:T(8,128)S(1)} %add.42), channel_id=1, source_target_pairs={{0,2},{1,3},{2,0},{3,1},{4,6},{5,7},{6,4},{7,5},{8,10},{9,11},{10,... | collective-permute-start | bytes 110600 | tf_op jit(solution)/shard_map/ppermute | solution.py:307
  35.2 12.4 %collective-permute-start.11 = (f32[72,128]{1,0:T(8,128)S(1)}, f32[72,128]{1,0:T(8,128)S(1)}, u32[]{:S(2)}, u32[]{:S(2)}) collective-permute-start(f32[72,128]{1,0:T(8,128)S(1)} %add_add_fusion.2), channel_id=1, source_target_pairs={{0,16},{1,17},{2,18},{3,19},{4,20},{5,21},{6,22},{7,23},{8,24},{9,... | collective-permute-start | bytes 110600 | tf_op jit(solution)/shard_map/ppermute | solution.py:307
  45.5 4.0 %collective-permute-start.10 = (f32[72,128]{1,0:T(8,128)S(1)}, f32[72,128]{1,0:T(8,128)S(1)}, u32[]{:S(2)}, u32[]{:S(2)}) collective-permute-start(f32[72,128]{1,0:T(8,128)S(1)} %add_add_fusion.2), channel_id=1, source_target_pairs={{0,24},{1,25},{2,26},{3,27},{4,28},{5,29},{6,30},{7,31},{8,16},{9,... | collective-permute-start | bytes 110600 | tf_op jit(solution)/shard_map/ppermute | solution.py:307
  45.5 4.0 %collective-permute-start.9 = (f32[72,128]{1,0:T(8,128)S(1)}, f32[72,128]{1,0:T(8,128)S(1)}, u32[]{:S(2)}, u32[]{:S(2)}) collective-permute-start(f32[72,128]{1,0:T(8,128)S(1)} %add_add_fusion.2), channel_id=1, source_target_pairs={{0,8},{1,9},{2,10},{3,11},{4,12},{5,13},{6,14},{7,15},{8,0},{9,1},... | collective-permute-start | bytes 110600 | tf_op jit(solution)/shard_map/ppermute | solution.py:307
  49.5 6.6 %collective-permute-start.14 = (f32[72,128]{1,0:T(8,128)S(1)}, f32[72,128]{1,0:T(8,128)S(1)}, u32[]{:S(2)}, u32[]{:S(2)}) collective-permute-start(f32[72,128]{1,0:T(8,128)S(1)} %add_add_fusion.1), channel_id=1, source_target_pairs={{0,192},{1,193},{2,194},{3,195},{4,196},{5,197},{6,198},{7,199},{8... | collective-permute-start | bytes 110600 | tf_op jit(solution)/shard_map/ppermute | solution.py:307
  53.4 5.2 %collective-permute-start.13 = (f32[72,128]{1,0:T(8,128)S(1)}, f32[72,128]{1,0:T(8,128)S(1)}, u32[]{:S(2)}, u32[]{:S(2)}) collective-permute-start(f32[72,128]{1,0:T(8,128)S(1)} %add_add_fusion.1), channel_id=1, source_target_pairs={{0,224},{1,225},{2,226},{3,227},{4,228},{5,229},{6,230},{7,231},{8... | collective-permute-start | bytes 110600 | tf_op jit(solution)/shard_map/ppermute | solution.py:307
  56.1 4.0 %collective-permute-start.12 = (f32[72,128]{1,0:T(8,128)S(1)}, f32[72,128]{1,0:T(8,128)S(1)}, u32[]{:S(2)}, u32[]{:S(2)}) collective-permute-start(f32[72,128]{1,0:T(8,128)S(1)} %add_add_fusion.1), channel_id=1, source_target_pairs={{0,32},{1,33},{2,34},{3,35},{4,36},{5,37},{6,38},{7,39},{8,40},{9,... | collective-permute-start | bytes 110600 | tf_op jit(solution)/shard_map/ppermute | solution.py:307
  60.0 7.2 %collective-permute-start.15 = (f32[72,128]{1,0:T(8,128)S(1)}, f32[72,128]{1,0:T(8,128)S(1)}, u32[]{:S(2)}, u32[]{:S(2)}) collective-permute-start(f32[72,128]{1,0:T(8,128)S(1)} %add_add_fusion), channel_id=1, source_target_pairs={{0,160},{1,161},{2,162},{3,163},{4,164},{5,165},{6,166},{7,167},{8... | collective-permute-start | bytes 110600 | tf_op jit(solution)/shard_map/ppermute | solution.py:307
